TPU v7x, 1024 devices: a whole 4x8x16 slice. The times are simulated.
1024 devices in a mesh: section: 16 (over y, x_hi), expert: 32 (over z, core), dp: 2 (over x_lo).
Axes of the slice: x: 4 (x_hi: 2, x_lo: 2; x = x_hi * 2 + x_lo), y: 8, z: 16, core: 2. Of those that a mesh axis runs over, the one named last changes fastest.
Arguments:
- grad_in: bfloat16 [2, 16, 4096, 3584], P(None, 'section', ('expert', 'dp')), may hold values from -6 to 6
- expert_ids: int32 [2, 16, 4096, 1], P(None, 'section', ('expert', 'dp')), may hold values from 0 to 31; in each aligned block of 64 rows (0 to 63, 64 to 127, ..., all dimensions but the last counted through in order) at most 3 rows name the same one
- gate_weights: float32 [16, 4096], P('section', ('expert', 'dp')), may hold values from 0.2 to 1
- back_rows: bfloat16 [16, 2, 32, 96, 3584], P('section', 'dp', 'expert'), may hold values from -6 to 6
- shared_down: bfloat16 [16, 1024, 3584], P('section', 'dp'), may hold values from -0.09375 to 0.09375
Outputs:
- dispatch_rows: bfloat16 [16, 2, 32, 96, 3584], P('section', 'dp', 'expert')
- section_grad: bfloat16 [16, 4096, 3584], P('section', ('expert', 'dp'))
- shared_grad: bfloat16 [2, 16, 4096, 1024], P(None, 'section', 'expert', 'dp')
Inputs may be any that keep to these rules, and one draw needn't show every extreme that they name: `expert_ids`: within the 64 tokens of one device block of one micro-batch and section, at most 3 tokens name the same expert, a bound that some block reaches.
All inputs are finite; a program needn't handle non-finite values.
Results may differ from a plain program's by a relative error of at most 0.001.
Values may be sent and summed in bfloat16 or wider, within the bound.
No kernel may reach another device: no remote copies, remote signals or barrier semaphores. Data moves between devices by JAX's collectives and lax.ppermute only.
A program may use at most 64 MiB of HBM per device.

v0:
```python
import jax
import jax.numpy as jnp
from jax import lax
from jax.sharding import PartitionSpec as P


def shifted(array, axis, by):
    peers = lax.axis_size(axis)
    pairs = [(i, i + by) for i in range(peers) if 0 <= i + by < peers]
    return lax.ppermute(array, axis, pairs)


def slot_positions(ident, groups, capacity):
    onehot = (ident[:, None] == jnp.arange(groups, dtype=jnp.int32)[None, :]).astype(jnp.int32)
    earlier = jnp.cumsum(onehot, axis=0) - onehot
    slot_index = jnp.sum(earlier * onehot, axis=1)
    return ident * capacity + slot_index


def on_device(grad_in, expert_ids, gate_weights, back_rows, shared_down):
    groups = lax.axis_size("expert")
    buffer_rows = back_rows.shape[3]
    capacity = buffer_rows // groups
    model_width = grad_in.shape[3]
    from_next = shifted(grad_in[0, 0], "section", -1)
    from_prev = shifted(grad_in[1, 0], "section", 1)
    row_range = jnp.arange(buffer_rows, dtype=jnp.int32)
    target_a = slot_positions(expert_ids[0, 0, :, 0], groups, capacity)
    target_b = slot_positions(expert_ids[1, 0, :, 0], groups, capacity)
    scaled = (gate_weights[0][:, None] * from_next.astype(jnp.float32)).astype(jnp.bfloat16)
    place_table = (row_range[:, None] == target_a[None, :]).astype(jnp.bfloat16)
    packed = jnp.dot(place_table, scaled, preferred_element_type=jnp.float32).astype(jnp.bfloat16)
    packed = packed.reshape(groups, capacity, model_width)
    outgoing = back_rows[0, 0, 0].reshape(groups, capacity, model_width)
    came_rows = lax.all_to_all(outgoing, "expert", split_axis=0, concat_axis=0, tiled=True)
    sent_rows = lax.all_to_all(packed, "expert", split_axis=0, concat_axis=0, tiled=True)
    pick_table = (target_b[:, None] == row_range[None, :]).astype(jnp.bfloat16)
    returned = jnp.dot(
        pick_table, came_rows.reshape(buffer_rows, model_width), preferred_element_type=jnp.float32
    )
    section_grad = (from_prev.astype(jnp.float32) + returned).astype(jnp.bfloat16)
    both_grads = jnp.stack([from_next, from_prev])
    down_part = shared_down[0]
    hidden_grad = jnp.einsum(
        "mtd,hd->mth",
        lax.all_gather(both_grads, "dp", axis=1, tiled=True),
        down_part,
        preferred_element_type=jnp.float32,
    ).astype(jnp.bfloat16)
    return (
        sent_rows.reshape(1, 1, 1, buffer_rows, model_width),
        section_grad[None],
        hidden_grad[:, None],
    )


def solution(mesh):
    placed = (
        P(None, "section", ("expert", "dp"), None),
        P(None, "section", ("expert", "dp"), None),
        P("section", ("expert", "dp")),
        P("section", "dp", "expert", None, None),
        P("section", "dp", None),
    )
    return jax.shard_map(
        on_device,
        mesh=mesh,
        in_specs=placed,
        out_specs=(
            P("section", "dp", "expert", None, None),
            P("section", ("expert", "dp"), None),
            P(None, "section", "expert", "dp"),
        ),
        check_vma=False,
    )
```

profile of v0, /device:TPU:56, one launch (start us, length us, event | category | flops | bytes accessed | tf_op | source)
XLA Modules:
  0.0 144.4 jit_solution(6258387816104336278)
XLA Ops:
  7.2 0.0 copy-start
  7.2 2.2 %reshape_squeeze.3 = bf16[32,3,3584]{2,1,0:T(4,128)(2,1)} reshape(bf16[1,1,1,96,3584]{4,3,2,1,0:T(8,128)(2,1)} %param.8) | data formatting | bytes 1376256 | tf_op jit(solution)/shard_map/reshape;squeeze | solution.py:34
  9.4 0.0 copy-start.1
  9.4 0.0 copy-start.2
  9.4 19.3 %all-to-all-start.1 = ((bf16[32,3,3584]{2,1,0:T(4,128)(2,1)}), bf16[32,3,3584]{2,1,0:T(4,128)(2,1)S(1)}, u32[]{:S(2)}, u32[]{:S(2)}) async-start(bf16[32,3,3584]{2,1,0:T(4,128)(2,1)} %reshape_squeeze.3), calls=%async_computation.1 | async-start | bytes 1835008 | tf_op jit(solution)/shard_map/all_to_all | solution.py:35
  28.7 0.0 copy-done
  28.7 0.8 slice_bitcast_fusion
  29.5 4.9 %collective-permute-start.1 = (bf16[64,3584]{1,0:T(8,128)(2,1)S(1)}, bf16[64,3584]{1,0:T(8,128)(2,1)S(1)}, u32[]{:S(2)}, u32[]{:S(2)}) collective-permute-start(bf16[64,3584]{1,0:T(8,128)(2,1)S(1)} %get-tuple-element.9), channel_id=1, source_target_pairs={{0,64},{64,128},{128,192},{192,256},{256,320},{320,384},{384,448},... | collective-permute-start | bytes 1376264 | tf_op jit(solution)/shard_map/ppermute | solution.py:10
  34.5 3.3 %collective-permute-start = (bf16[64,3584]{1,0:T(8,128)(2,1)}, bf16[64,3584]{1,0:T(8,128)(2,1)S(1)}, u32[]{:S(2)}, u32[]{:S(2)}) collective-permute-start(bf16[64,3584]{1,0:T(8,128)(2,1)} %get-tuple-element.10), channel_id=1, source_target_pairs={{64,0},{128,64},{192,128},{256,192},{320,256},{384,320},{448,384},... | collective-permute-start | bytes 1376264 | tf_op jit(solution)/shard_map/ppermute | solution.py:10
  37.8 0.0 copy-done.1
  37.8 0.1 fusion.10
  37.9 0.1 reduce_window_sum.18
  38.0 0.1 fusion.11
  38.0 0.1 reduce_window_sum.17
  38.1 0.2 select_reduce_fusion
  38.3 18.0 %collective-permute-done = bf16[64,3584]{1,0:T(8,128)(2,1)S(1)} collective-permute-done((bf16[64,3584]{1,0:T(8,128)(2,1)}, bf16[64,3584]{1,0:T(8,128)(2,1)S(1)}, u32[]{:S(2)}, u32[]{:S(2)}) %collective-permute-start) | collective-permute-done | bytes 458784 | tf_op jit(solution)/shard_map/ppermute | solution.py:10
  56.3 0.0 copy-done.2
  56.3 0.4 convolution_convert_fusion
  56.8 1.2 reshape.34
  57.9 21.2 %all-to-all-done.1 = bf16[32,3,3584]{2,1,0:T(4,128)(2,1)S(1)} async-done(((bf16[32,3,3584]{2,1,0:T(4,128)(2,1)}), bf16[32,3,3584]{2,1,0:T(4,128)(2,1)S(1)}, u32[]{:S(2)}, u32[]{:S(2)}) %all-to-all-start.1) | async-done | bytes 688160 | tf_op jit(solution)/shard_map/all_to_all | solution.py:35
  79.1 3.9 %all-to-all-start = ((bf16[32,3,3584]{2,1,0:T(4,128)(2,1)}), bf16[32,3,3584]{2,1,0:T(4,128)(2,1)S(1)}, u32[]{:S(2)}, u32[]{:S(2)}) async-start(bf16[32,3,3584]{2,1,0:T(4,128)(2,1)} %reshape.34), calls=%async_computation | async-start | bytes 1835008 | tf_op jit(solution)/shard_map/all_to_all | solution.py:36
  83.1 0.0 all-gather.2.cloned.1.call-start
  83.1 0.0 collective-permute-done.1
  83.1 1.0 pad_maximum_fusion
  84.1 0.0 all-gather.2.cloned.1.call-update
  84.2 46.0 %all-gather.2.cloned.1.call-done = bf16[2,128,3584]{2,1,0:T(8,128)(2,1)} async-done(((bf16[2,64,3584]{2,1,0:T(8,128)(2,1)}), bf16[2,128,3584]{2,1,0:T(8,128)(2,1)}) %all-gather.2.cloned.1.call-update) | async-done | bytes 1835024 | tf_op jit(solution)/shard_map/all_gather | solution.py:46
  130.1 4.4 %fusion.5 = bf16[2,1,128,512]{3,2,1,0:T(8,128)(2,1)} fusion(bf16[2,128,3584]{2,1,0:T(8,128)(2,1)} %all-gather.2.cloned.1.call-done, bf16[1,512,3584]{2,1,0:T(8,128)(2,1)} %param.9), kind=kOutput, calls=%fused_computation.4 | convolution fusion | flops 939655168 | bytes 5767168 | tf_op jit(solution)/shard_map/mtd,hd->mth/dot_general | solution.py:44
  134.6 0.6 reshape.36
  135.2 1.1 fusion.8
  136.3 0.0 all-to-all-done
  136.3 1.3 reshape.35
  (2 shorter events, 0.0 us)
Async XLA Ops:
  7.2 21.5 %copy-start = (bf16[2,1,64,3584]{3,2,1,0:T(8,128)(2,1)S(1)}, bf16[2,1,64,3584]{3,2,1,0:T(8,128)(2,1)}, u32[]{:S(2)}) copy-start(bf16[2,1,64,3584]{3,2,1,0:T(8,128)(2,1)} %param.5) | copy-start | bytes 2752516
  9.4 28.4 %copy-start.1 = (s32[2,1,64,1]{2,3,1,0:T(1,128)S(1)}, s32[2,1,64,1]{2,3,1,0:T(1,128)}, u32[]{:S(2)}) copy-start(s32[2,1,64,1]{2,3,1,0:T(1,128)} %param.6) | copy-start | bytes 1540
  9.4 46.9 %copy-start.2 = (f32[1,64]{1,0:T(1,128)S(1)}, f32[1,64]{1,0:T(1,128)}, u32[]{:S(2)}) copy-start(f32[1,64]{1,0:T(1,128)} %param.7) | copy-start | bytes 772
  9.4 69.7 %all-to-all-start.1 = ((bf16[32,3,3584]{2,1,0:T(4,128)(2,1)}), bf16[32,3,3584]{2,1,0:T(4,128)(2,1)S(1)}, u32[]{:S(2)}, u32[]{:S(2)}) async-start(bf16[32,3,3584]{2,1,0:T(4,128)(2,1)} %reshape_squeeze.3), calls=%async_computation.1 | async-start | bytes 1835008 | tf_op jit(solution)/shard_map/all_to_all | solution.py:35
  29.5 53.6 %collective-permute-start.1 = (bf16[64,3584]{1,0:T(8,128)(2,1)S(1)}, bf16[64,3584]{1,0:T(8,128)(2,1)S(1)}, u32[]{:S(2)}, u32[]{:S(2)}) collective-permute-start(bf16[64,3584]{1,0:T(8,128)(2,1)S(1)} %get-tuple-element.9), channel_id=1, source_target_pairs={{0,64},{64,128},{128,192},{192,256},{256,320},{320,384},{384,448},... | collective-permute-start | bytes 1376264 | tf_op jit(solution)/shard_map/ppermute | solution.py:10
  34.5 21.9 %collective-permute-start = (bf16[64,3584]{1,0:T(8,128)(2,1)}, bf16[64,3584]{1,0:T(8,128)(2,1)S(1)}, u32[]{:S(2)}, u32[]{:S(2)}) collective-permute-start(bf16[64,3584]{1,0:T(8,128)(2,1)} %get-tuple-element.10), channel_id=1, source_target_pairs={{64,0},{128,64},{192,128},{256,192},{320,256},{384,320},{448,384},... | collective-permute-start | bytes 1376264 | tf_op jit(solution)/shard_map/ppermute | solution.py:10
  79.1 57.1 %all-to-all-start = ((bf16[32,3,3584]{2,1,0:T(4,128)(2,1)}), bf16[32,3,3584]{2,1,0:T(4,128)(2,1)S(1)}, u32[]{:S(2)}, u32[]{:S(2)}) async-start(bf16[32,3,3584]{2,1,0:T(4,128)(2,1)} %reshape.34), calls=%async_computation | async-start | bytes 1835008 | tf_op jit(solution)/shard_map/all_to_all | solution.py:36
  83.1 47.0 %all-gather.2.cloned.1.call-start = ((), (), s32[]{:S(2)}) async-start(), calls=%async_computation.2 | async-start | bytes 2752512 | tf_op jit(solution)/shard_map/all_gather | solution.py:46
Sparse Core Ops, SparseCore 0:
  86.6 43.4 all-gather.1
where the time goes:
time: 146 us; the launch traced here: 144 us
  waiting for transfers between devices  85.2 us (58%)
  starting transfers between devices  31.5 us (22%)
  between operations  14.1 us (10%)
  local copies, waits for them, and re-layouts  6.16 us (4%)
  matrix products  5.94 us (4%)
  other arithmetic  1.54 us (1%)
    all_gather x1, waiting for transfers between devices, on_device(): lax.all_gather(both_grads, 'dp', axis=1, tiled=True)  46 us
    all_to_all x1, waiting for transfers between devices, on_device(): lax.all_to_all(outgoing, 'expert', split_axis=0, concat_axis=0, tiled=True)  21.2 us
    all_to_all x1, starting transfers between devices, on_device(): lax.all_to_all(outgoing, 'expert', split_axis=0, concat_axis=0, tiled=True)  19.3 us
    ppermute x2, waiting for transfers between devices, shifted(): return lax.ppermute(array, axis, pairs)  18 us
    ppermute x2, starting transfers between devices, shifted(): return lax.ppermute(array, axis, pairs)  8.23 us
    dot_general x1, matrix products, on_device(): jnp.einsum('mtd,hd->mth', lax.all_gather(both_grads, 'dp', axis=1, tiled=...  4.44 us
    all_to_all x1, starting transfers between devices, on_device(): lax.all_to_all(packed, 'expert', split_axis=0, concat_axis=0, tiled=True)  3.92 us
  transfers between devices with their start and end apart: 5, of which 3 were waited for; matrix products, arithmetic and copies ran while one was open for 7% of the time, Pallas kernels for 0%

commit v1 on v0

v1 whole, which is shorter than its diff:
```python
import jax
import jax.numpy as jnp
from jax import lax
from jax.sharding import PartitionSpec as P

CORES = 2
PARTS = 4


def shifted(array, axis, by):
    peers = lax.axis_size(axis)
    pairs = [(i, i + by) for i in range(peers) if 0 <= i + by < peers]
    return lax.ppermute(array, axis, pairs)


def swapped(array, axis):
    peers = lax.axis_size(axis)
    return lax.ppermute(array, axis, [(i, i ^ 1) for i in range(peers)])


def slot_of(ident):
    same = ident[:, None] == ident[None, :]
    count = ident.shape[0]
    order = jnp.arange(count, dtype=jnp.int32)
    before = order[None, :] < order[:, None]
    return jnp.sum((same & before).astype(jnp.int32), axis=1)


def select(rows, width, dtype=jnp.bfloat16):
    return (rows[:, None] == jnp.arange(width, dtype=jnp.int32)[None, :]).astype(dtype)


def on_device(grad_in, expert_ids, gate_weights, back_rows, shared_down):
    hosts = lax.axis_size("expert")
    chips = hosts // CORES
    core = lax.axis_index("expert") % CORES
    other = 1 - core
    buffer_rows, width = back_rows.shape[3:]
    cap = buffer_rows // hosts
    chip_rows = CORES * cap
    part = width // PARTS
    across = [[CORES * z + c for z in range(chips)] for c in range(CORES)]

    def exchanged(pieces):
        return lax.all_to_all(
            pieces, "expert", split_axis=0, concat_axis=0, tiled=True, axis_index_groups=across
        )

    came = exchanged(back_rows[0, 0, 0].reshape(chips, chip_rows * PARTS, part))
    came = came.reshape(buffer_rows, width)

    from_next = shifted(grad_in[0, 0], "section", -1)
    from_prev = shifted(grad_in[1, 0], "section", 1)
    ident_a = expert_ids[0, 0, :, 0]
    ident_b = expert_ids[1, 0, :, 0]
    ident_mate = swapped(ident_a, "expert")

    scaled = (gate_weights[0][:, None] * from_next.astype(jnp.float32)).astype(jnp.bfloat16)
    scaled_mate = swapped(scaled, "expert")
    chip_tokens = jnp.concatenate([scaled, scaled_mate], axis=0)

    def place(ident, source):
        row = (ident // CORES) * chip_rows + source * cap + slot_of(ident)
        return jnp.where(ident % CORES == core, row, buffer_rows)

    target = jnp.concatenate([place(ident_a, core), place(ident_mate, other)])
    table = (jnp.arange(buffer_rows, dtype=jnp.int32)[:, None] == target[None, :]).astype(jnp.bfloat16)
    packed = jnp.dot(table, chip_tokens, preferred_element_type=jnp.float32).astype(jnp.bfloat16)
    sent = exchanged(packed.reshape(chips, chip_rows * PARTS, part)).reshape(buffer_rows, width)

    lines = jnp.arange(chips * cap, dtype=jnp.int32)
    passed = select((lines // cap) * chip_rows + other * cap + lines % cap, buffer_rows)
    passed = jnp.dot(passed, came, preferred_element_type=jnp.float32).astype(jnp.bfloat16)
    passed = swapped(passed, "expert")
    slot_b = slot_of(ident_b)
    here = ident_b % CORES == core
    from_own = jnp.where(here, (ident_b // CORES) * chip_rows + core * cap + slot_b, buffer_rows)
    from_mate = jnp.where(here, chips * cap, (ident_b // CORES) * cap + slot_b)
    returned = jnp.dot(
        select(from_own, buffer_rows), came, preferred_element_type=jnp.float32
    ) + jnp.dot(select(from_mate, chips * cap), passed, preferred_element_type=jnp.float32)
    section_grad = (from_prev.astype(jnp.float32) + returned).astype(jnp.bfloat16)

    replica = lax.axis_index("dp")
    down_part = shared_down[0]

    def hidden(own):
        mate = swapped(own, "dp")
        first = jnp.where(replica == 0, own, mate)
        second = jnp.where(replica == 0, mate, own)
        tokens = jnp.concatenate([first, second], axis=0)
        return jnp.einsum(
            "td,hd->th", tokens, down_part, preferred_element_type=jnp.float32
        ).astype(jnp.bfloat16)

    hidden_grad = jnp.stack([hidden(from_next), hidden(from_prev)])
    return (
        sent.reshape(1, 1, 1, buffer_rows, width),
        section_grad[None],
        hidden_grad[:, None],
    )


def solution(mesh):
    placed = (
        P(None, "section", ("expert", "dp"), None),
        P(None, "section", ("expert", "dp"), None),
        P("section", ("expert", "dp")),
        P("section", "dp", "expert", None, None),
        P("section", "dp", None),
    )
    return jax.shard_map(
        on_device,
        mesh=mesh,
        in_specs=placed,
        out_specs=(
            P("section", "dp", "expert", None, None),
            P("section", ("expert", "dp"), None),
            P(None, "section", "expert", "dp"),
        ),
        check_vma=False,
    )
```

time: 146 us -> 111 us (0.76)
  waiting for transfers between devices: 85.2 us -> 41.5 us
  starting transfers between devices: 31.5 us -> 50.4 us
  between operations: 14.1 us -> 0.88 us
  other arithmetic: 1.54 us -> 3.7 us
    all_gather x1 -> x0, waiting for transfers between devices: 46 us -> none  [on_device(): lax.all_gather(both_grads, 'dp', axis=1, tiled=True)]
    ppermute x0 -> x5, starting transfers between devices: none -> 11.6 us  [swapped(): return lax.ppermute(array, axis, [(i, i ^ 1) for i in range(peers)])]
    all_to_all x2, starting transfers between devices: 23.2 us -> 30.5 us  [exchanged(): lax.all_to_all(pieces, 'expert', split_axis=0, concat_axis=0, tiled=True,...]
    select_n x0 -> x5, other arithmetic: none -> 2.21 us  [the longest x2 2.17 us: hidden(): first = jnp.where(replica == 0, own, mate)]
    reshape x3 -> x2, local copies, waits for them, and re-layouts: 3.1 us -> 1.67 us  [the longest x1 1.26 us: on_device(): packed.reshape(chips, chip_rows * PARTS, part)]
    another operation x1 -> x2, local copies, waits for them, and re-layouts: 2.22 us -> 3.54 us  [the longest x1 2.28 us: on_device(): came = exchanged(back_rows[0, 0, 0].reshape(chips, chip_rows * PARTS, part))]
    dot_general x3 -> x6, matrix products: 5.94 us -> 6.82 us  [the longest x2 4.76 us: hidden(): jnp.einsum('td,hd->th', tokens, down_part, preferred_element_type=jnp.flo...]
  transfers between devices with their start and end apart: 5 -> 9, of which waited for: 3 -> 5; matrix products, arithmetic and copies ran while one was open for 7% -> 13% of each run, Pallas kernels for 0% -> 0%
where the time goes in v1:
time: 111 us; the launch traced here: 109 us
  starting transfers between devices  50.4 us (45%)
  waiting for transfers between devices  41.5 us (37%)
  matrix products  6.82 us (6%)
  local copies, waits for them, and re-layouts  6.04 us (5%)
  other arithmetic  3.7 us (3%)
    all_to_all x2, starting transfers between devices, exchanged(): lax.all_to_all(pieces, 'expert', split_axis=0, concat_axis=0, tiled=True,...  30.5 us
    all_to_all x2, waiting for transfers between devices, exchanged(): lax.all_to_all(pieces, 'expert', split_axis=0, concat_axis=0, tiled=True,...  22 us
    ppermute x2, waiting for transfers between devices, shifted(): return lax.ppermute(array, axis, pairs)  18.1 us
    ppermute x5, starting transfers between devices, swapped(): return lax.ppermute(array, axis, [(i, i ^ 1) for i in range(peers)])  11.6 us
    ppermute x2, starting transfers between devices, shifted(): return lax.ppermute(array, axis, pairs)  8.25 us
    dot_general x2, matrix products, hidden(): jnp.einsum('td,hd->th', tokens, down_part, preferred_element_type=jnp.flo...  4.76 us
    another operation x1, local copies, waits for them, and re-layouts, on_device(): came = exchanged(back_rows[0, 0, 0].reshape(chips, chip_rows * PARTS, part))  2.28 us
  transfers between devices with their start and end apart: 9, of which 5 were waited for; matrix products, arithmetic and copies ran while one was open for 13% of the time, Pallas kernels for 0%

profile of v1, /device:TPU:56, one launch (start us, length us, event | category | flops | bytes accessed | tf_op | source)
XLA Modules:
  0.0 109.3 jit_solution(5916988950423792042)
XLA Ops:
  0.6 0.0 copy-start
  0.6 0.8 slice_bitcast_fusion.2
  1.4 1.9 %collective-permute-start = (s32[64]{0:T(128)S(1)}, s32[64]{0:T(128)S(1)}, u32[]{:S(2)}, u32[]{:S(2)}) collective-permute-start(s32[64]{0:T(128)S(1)} %get-tuple-element.20), channel_id=1, source_target_pairs={{0,2},{2,0},{4,6},{6,4},{8,10},{10,8},{12,14},{14,12},{16,18},{18,... | collective-permute-start | bytes 776 | tf_op jit(solution)/shard_map/ppermute | solution.py:18
  3.3 2.3 %reshape_squeeze.3 = bf16[16,24,896]{2,1,0:T(8,128)(2,1)} reshape(bf16[1,1,1,96,3584]{4,3,2,1,0:T(8,128)(2,1)} %param.8) | data formatting | bytes 1376256 | tf_op jit(solution)/shard_map/reshape;squeeze | solution.py:49
  5.6 0.0 copy-start.1
  5.6 0.0 copy-start.2
  5.6 19.0 %all-to-all-start.1 = ((bf16[16,24,896]{2,1,0:T(8,128)(2,1)}), bf16[16,24,896]{2,1,0:T(8,128)(2,1)S(1)}, u32[]{:S(2)}, u32[]{:S(2)}) async-start(bf16[16,24,896]{2,1,0:T(8,128)(2,1)} %reshape_squeeze.3), calls=%async_computation.1 | async-start | bytes 1376256 | tf_op jit(solution)/shard_map/all_to_all | solution.py:45
  24.6 0.0 copy-done
  24.6 0.1 slice_bitcast_fusion
  24.7 4.9 %collective-permute-start.3 = (bf16[64,3584]{1,0:T(8,128)(2,1)S(1)}, bf16[64,3584]{1,0:T(8,128)(2,1)S(1)}, u32[]{:S(2)}, u32[]{:S(2)}) collective-permute-start(bf16[64,3584]{1,0:T(8,128)(2,1)S(1)} %get-tuple-element.16), channel_id=1, source_target_pairs={{0,64},{64,128},{128,192},{192,256},{256,320},{320,384},{384,448},... | collective-permute-start | bytes 1376264 | tf_op jit(solution)/shard_map/ppermute | solution.py:13
  29.6 3.3 %collective-permute-start.1 = (bf16[64,3584]{1,0:T(8,128)(2,1)S(1)}, bf16[64,3584]{1,0:T(8,128)(2,1)S(1)}, u32[]{:S(2)}, u32[]{:S(2)}) collective-permute-start(bf16[64,3584]{1,0:T(8,128)(2,1)S(1)} %get-tuple-element.17), channel_id=1, source_target_pairs={{64,0},{128,64},{192,128},{256,192},{320,256},{384,320},{448,384},... | collective-permute-start | bytes 1376264 | tf_op jit(solution)/shard_map/ppermute | solution.py:13
  32.9 0.2 convert_reduce_fusion.2
  33.1 0.2 convert_reduce_fusion
  33.3 0.0 copy-done.1
  33.4 18.1 %collective-permute-done.1 = bf16[64,3584]{1,0:T(8,128)(2,1)S(1)} collective-permute-done((bf16[64,3584]{1,0:T(8,128)(2,1)S(1)}, bf16[64,3584]{1,0:T(8,128)(2,1)S(1)}, u32[]{:S(2)}, u32[]{:S(2)}) %collective-permute-start.1) | collective-permute-done | bytes 458784 | tf_op jit(solution)/shard_map/ppermute | solution.py:13
  51.5 0.0 copy-done.2
  51.5 0.1 multiply_convert_fusion
  51.6 1.9 %collective-permute-start.2 = (bf16[64,3584]{1,0:T(8,128)(2,1)S(1)}, bf16[64,3584]{1,0:T(8,128)(2,1)S(1)}, u32[]{:S(2)}, u32[]{:S(2)}) collective-permute-start(bf16[64,3584]{1,0:T(8,128)(2,1)S(1)} %multiply_convert_fusion), channel_id=1, source_target_pairs={{0,2},{2,0},{4,6},{6,4},{8,10},{10,8},{12,14},{14,12},{16,18},{18,... | collective-permute-start | bytes 1376264 | tf_op jit(solution)/shard_map/ppermute | solution.py:18
  53.6 0.0 collective-permute-done
  53.6 0.2 convert_reduce_fusion.1
  53.7 0.0 collective-permute-done.3
  53.8 3.4 %collective-permute-start.6 = (bf16[64,3584]{1,0:T(8,128)(2,1)S(1)}, bf16[64,3584]{1,0:T(8,128)(2,1)}, u32[]{:S(2)}, u32[]{:S(2)}) collective-permute-start(bf16[64,3584]{1,0:T(8,128)(2,1)S(1)} %collective-permute-done.3), channel_id=1, source_target_pairs={{0,1},{1,0},{2,3},{3,2},{4,5},{5,4},{6,7},{7,6},{8,9},{9,8},{10,11... | collective-permute-start | bytes 1376264 | tf_op jit(solution)/shard_map/ppermute | solution.py:18
  57.2 0.1 pad_add_fusion
  57.3 2.4 %collective-permute-start.5 = (bf16[64,3584]{1,0:T(8,128)(2,1)S(1)}, bf16[64,3584]{1,0:T(8,128)(2,1)}, u32[]{:S(2)}, u32[]{:S(2)}) collective-permute-start(bf16[64,3584]{1,0:T(8,128)(2,1)S(1)} %collective-permute-done.1), channel_id=1, source_target_pairs={{0,1},{1,0},{2,3},{3,2},{4,5},{5,4},{6,7},{7,6},{8,9},{9,8},{10,11... | collective-permute-start | bytes 1376264 | tf_op jit(solution)/shard_map/ppermute | solution.py:18
  59.7 0.0 collective-permute-done.2
  59.7 0.3 convolution_convert_fusion
  60.1 1.3 %reshape.115 = bf16[16,24,896]{2,1,0:T(8,128)(2,1)} reshape(bf16[96,3584]{1,0:T(8,128)(2,1)S(1)} %convolution_convert_fusion) | data formatting | bytes 1376256 | tf_op jit(solution)/shard_map/reshape | solution.py:69
  61.3 0.2 all-to-all-done.1
  61.5 11.5 %all-to-all-start = ((bf16[16,24,896]{2,1,0:T(8,128)(2,1)}), bf16[16,24,896]{2,1,0:T(8,128)(2,1)S(1)}, u32[]{:S(2)}, u32[]{:S(2)}) async-start(bf16[16,24,896]{2,1,0:T(8,128)(2,1)} %reshape.115), calls=%async_computation | async-start | bytes 1376256 | tf_op jit(solution)/shard_map/all_to_all | solution.py:45
  73.1 0.0 collective-permute-done.6
  73.1 1.1 broadcast_select_fusion.1
  74.2 0.0 copy-start.3
  74.2 3.5 %fusion.10 = bf16[1,128,512]{2,1,0:T(8,128)(2,1)S(1)} fusion(bf16[1,512,3584]{2,1,0:T(8,128)(2,1)} %param.9, bf16[64,3584]{1,0:T(8,128)(2,1)S(1)} %get-tuple-element.15, bf16[64,3584]{1,0:T(8,128)(2,1)S(1)} %get-tuple-element.14), kind=kOutput, calls=%fused_computation.9 | convolution fusion | flops 471662592 | bytes 4718592 | tf_op jit(solution)/shard_map/td,hd->th/dot_general | solution.py:92
  77.7 0.8 collective-permute-done.5
  78.5 1.1 broadcast_select_fusion.3
  79.6 0.0 copy-done.3
  79.6 1.3 %fusion.13 = bf16[1,128,512]{2,1,0:T(8,128)(2,1)S(1)} fusion(bf16[1,512,3584]{2,1,0:T(8,128)(2,1)S(1)} %copy-done.3, bf16[64,3584]{1,0:T(8,128)(2,1)S(1)} %get-tuple-element.13, bf16[64,3584]{1,0:T(8,128)(2,1)S(1)} %get-tuple-element.12), kind=kOutput, calls=%fused_computation.10 | convolution fusion | flops 471662592 | bytes 4718592 | tf_op jit(solution)/shard_map/td,hd->th/dot_general | solution.py:92
  80.9 0.4 reshape.116
  81.3 0.3 convolution_convert_fusion.1
  81.6 1.9 %collective-permute-start.4 = (bf16[48,3584]{1,0:T(8,128)(2,1)S(1)}, bf16[48,3584]{1,0:T(8,128)(2,1)S(1)}, u32[]{:S(2)}, u32[]{:S(2)}) collective-permute-start(bf16[48,3584]{1,0:T(8,128)(2,1)S(1)} %convolution_convert_fusion.1), channel_id=1, source_target_pairs={{0,2},{2,0},{4,6},{6,4},{8,10},{10,8},{12,14},{14,12},{16,18},{18,... | collective-permute-start | bytes 1032200 | tf_op jit(solution)/shard_map/ppermute | solution.py:18
  83.5 0.7 maximum_bitcast_fusion
  84.3 0.3 fusion.29
  84.6 0.6 collective-permute-done.4
  85.2 1.1 %fusion.25 = bf16[1,64,3584]{2,1,0:T(8,128)(2,1)} fusion(bf16[64,3584]{1,0:T(8,128)(2,1)S(1)} %collective-permute-done.3, f32[64,3584]{1,0:T(8,128)S(1)} %fusion.29, bf16[48,3584]{1,0:T(8,128)(2,1)S(1)} %collective-permute-done.4, s32[64]{0:T(128)S(1)} %get-tuple-element.9), kind=kOutput, calls=%fused_computation.22 | convolution fusion | flops 22940672 | bytes 2179328 | tf_op jit(solution)/shard_map/dot_general | solution.py:81
  86.3 21.8 %all-to-all-done = bf16[16,24,896]{2,1,0:T(8,128)(2,1)S(1)} async-done(((bf16[16,24,896]{2,1,0:T(8,128)(2,1)}), bf16[16,24,896]{2,1,0:T(8,128)(2,1)S(1)}, u32[]{:S(2)}, u32[]{:S(2)}) %all-to-all-start) | async-done | bytes 688160 | tf_op jit(solution)/shard_map/all_to_all | solution.py:45
  108.1 1.3 %reshape_reshape.3 = bf16[1,1,1,96,3584]{4,3,2,1,0:T(8,128)(2,1)} reshape(bf16[16,24,896]{2,1,0:T(8,128)(2,1)S(1)} %all-to-all-done) | data formatting | bytes 1376256 | tf_op jit(solution)/shard_map/reshape;reshape | solution.py:98
  (4 shorter events, 0.1 us)
Async XLA Ops:
  0.6 24.0 %copy-start = (bf16[2,1,64,3584]{3,2,1,0:T(8,128)(2,1)S(1)}, bf16[2,1,64,3584]{3,2,1,0:T(8,128)(2,1)}, u32[]{:S(2)}) copy-start(bf16[2,1,64,3584]{3,2,1,0:T(8,128)(2,1)} %param.5) | copy-start | bytes 2752516
  1.4 52.2 %collective-permute-start = (s32[64]{0:T(128)S(1)}, s32[64]{0:T(128)S(1)}, u32[]{:S(2)}, u32[]{:S(2)}) collective-permute-start(s32[64]{0:T(128)S(1)} %get-tuple-element.20), channel_id=1, source_target_pairs={{0,2},{2,0},{4,6},{6,4},{8,10},{10,8},{12,14},{14,12},{16,18},{18,... | collective-permute-start | bytes 776 | tf_op jit(solution)/shard_map/ppermute | solution.py:18
  5.6 27.7 %copy-start.1 = (s32[2,1,64,1]{2,3,1,0:T(1,128)S(1)}, s32[2,1,64,1]{2,3,1,0:T(1,128)}, u32[]{:S(2)}) copy-start(s32[2,1,64,1]{2,3,1,0:T(1,128)} %param.6) | copy-start | bytes 1540
  5.6 45.9 %copy-start.2 = (f32[1,64]{1,0:T(1,128)S(1)}, f32[1,64]{1,0:T(1,128)}, u32[]{:S(2)}) copy-start(f32[1,64]{1,0:T(1,128)} %param.7) | copy-start | bytes 772
  5.6 55.9 %all-to-all-start.1 = ((bf16[16,24,896]{2,1,0:T(8,128)(2,1)}), bf16[16,24,896]{2,1,0:T(8,128)(2,1)S(1)}, u32[]{:S(2)}, u32[]{:S(2)}) async-start(bf16[16,24,896]{2,1,0:T(8,128)(2,1)} %reshape_squeeze.3), calls=%async_computation.1 | async-start | bytes 1376256 | tf_op jit(solution)/shard_map/all_to_all | solution.py:45
  24.7 29.1 %collective-permute-start.3 = (bf16[64,3584]{1,0:T(8,128)(2,1)S(1)}, bf16[64,3584]{1,0:T(8,128)(2,1)S(1)}, u32[]{:S(2)}, u32[]{:S(2)}) collective-permute-start(bf16[64,3584]{1,0:T(8,128)(2,1)S(1)} %get-tuple-element.16), channel_id=1, source_target_pairs={{0,64},{64,128},{128,192},{192,256},{256,320},{320,384},{384,448},... | collective-permute-start | bytes 1376264 | tf_op jit(solution)/shard_map/ppermute | solution.py:13
  29.6 21.8 %collective-permute-start.1 = (bf16[64,3584]{1,0:T(8,128)(2,1)S(1)}, bf16[64,3584]{1,0:T(8,128)(2,1)S(1)}, u32[]{:S(2)}, u32[]{:S(2)}) collective-permute-start(bf16[64,3584]{1,0:T(8,128)(2,1)S(1)} %get-tuple-element.17), channel_id=1, source_target_pairs={{64,0},{128,64},{192,128},{256,192},{320,256},{384,320},{448,384},... | collective-permute-start | bytes 1376264 | tf_op jit(solution)/shard_map/ppermute | solution.py:13
  51.6 8.1 %collective-permute-start.2 = (bf16[64,3584]{1,0:T(8,128)(2,1)S(1)}, bf16[64,3584]{1,0:T(8,128)(2,1)S(1)}, u32[]{:S(2)}, u32[]{:S(2)}) collective-permute-start(bf16[64,3584]{1,0:T(8,128)(2,1)S(1)} %multiply_convert_fusion), channel_id=1, source_target_pairs={{0,2},{2,0},{4,6},{6,4},{8,10},{10,8},{12,14},{14,12},{16,18},{18,... | collective-permute-start | bytes 1376264 | tf_op jit(solution)/shard_map/ppermute | solution.py:18
  53.8 19.3 %collective-permute-start.6 = (bf16[64,3584]{1,0:T(8,128)(2,1)S(1)}, bf16[64,3584]{1,0:T(8,128)(2,1)}, u32[]{:S(2)}, u32[]{:S(2)}) collective-permute-start(bf16[64,3584]{1,0:T(8,128)(2,1)S(1)} %collective-permute-done.3), channel_id=1, source_target_pairs={{0,1},{1,0},{2,3},{3,2},{4,5},{5,4},{6,7},{7,6},{8,9},{9,8},{10,11... | collective-permute-start | bytes 1376264 | tf_op jit(solution)/shard_map/ppermute | solution.py:18
  57.3 21.2 %collective-permute-start.5 = (bf16[64,3584]{1,0:T(8,128)(2,1)S(1)}, bf16[64,3584]{1,0:T(8,128)(2,1)}, u32[]{:S(2)}, u32[]{:S(2)}) collective-permute-start(bf16[64,3584]{1,0:T(8,128)(2,1)S(1)} %collective-permute-done.1), channel_id=1, source_target_pairs={{0,1},{1,0},{2,3},{3,2},{4,5},{5,4},{6,7},{7,6},{8,9},{9,8},{10,11... | collective-permute-start | bytes 1376264 | tf_op jit(solution)/shard_map/ppermute | solution.py:18
  61.5 46.6 %all-to-all-start = ((bf16[16,24,896]{2,1,0:T(8,128)(2,1)}), bf16[16,24,896]{2,1,0:T(8,128)(2,1)S(1)}, u32[]{:S(2)}, u32[]{:S(2)}) async-start(bf16[16,24,896]{2,1,0:T(8,128)(2,1)} %reshape.115), calls=%async_computation | async-start | bytes 1376256 | tf_op jit(solution)/shard_map/all_to_all | solution.py:45
  74.2 5.4 %copy-start.3 = (bf16[1,512,3584]{2,1,0:T(8,128)(2,1)S(1)}, bf16[1,512,3584]{2,1,0:T(8,128)(2,1)}, u32[]{:S(2)}) copy-start(bf16[1,512,3584]{2,1,0:T(8,128)(2,1)} %param.9) | copy-start | bytes 11010052
  81.6 3.5 %collective-permute-start.4 = (bf16[48,3584]{1,0:T(8,128)(2,1)S(1)}, bf16[48,3584]{1,0:T(8,128)(2,1)S(1)}, u32[]{:S(2)}, u32[]{:S(2)}) collective-permute-start(bf16[48,3584]{1,0:T(8,128)(2,1)S(1)} %convolution_convert_fusion.1), channel_id=1, source_target_pairs={{0,2},{2,0},{4,6},{6,4},{8,10},{10,8},{12,14},{14,12},{16,18},{18,... | collective-permute-start | bytes 1032200 | tf_op jit(solution)/shard_map/ppermute | solution.py:18

commit v2 on v1

--- a/solution.py
+++ b/solution.py
@@ -46,14 +46,17 @@
             pieces, "expert", split_axis=0, concat_axis=0, tiled=True, axis_index_groups=across
         )
 
-    came = exchanged(back_rows[0, 0, 0].reshape(chips, chip_rows * PARTS, part))
+    pieces = back_rows[0, 0, 0].reshape(chips, chip_rows * PARTS, part)
+    pieces, own_a = lax.optimization_barrier((pieces, grad_in[0, 0]))
+    came = exchanged(pieces)
     came = came.reshape(buffer_rows, width)
 
-    from_next = shifted(grad_in[0, 0], "section", -1)
-    from_prev = shifted(grad_in[1, 0], "section", 1)
+    from_next = shifted(own_a, "section", -1)
     ident_a = expert_ids[0, 0, :, 0]
     ident_b = expert_ids[1, 0, :, 0]
-    ident_mate = swapped(ident_a, "expert")
+    own_ident, own_b, from_next = lax.optimization_barrier((ident_a, grad_in[1, 0], from_next))
+    from_prev = shifted(own_b, "section", 1)
+    ident_mate = swapped(own_ident, "expert")
 
     scaled = (gate_weights[0][:, None] * from_next.astype(jnp.float32)).astype(jnp.bfloat16)
     scaled_mate = swapped(scaled, "expert")
@@ -66,6 +69,7 @@
     target = jnp.concatenate([place(ident_a, core), place(ident_mate, other)])
     table = (jnp.arange(buffer_rows, dtype=jnp.int32)[:, None] == target[None, :]).astype(jnp.bfloat16)
     packed = jnp.dot(table, chip_tokens, preferred_element_type=jnp.float32).astype(jnp.bfloat16)
+    from_prev, came = lax.optimization_barrier((from_prev, came))
     sent = exchanged(packed.reshape(chips, chip_rows * PARTS, part)).reshape(buffer_rows, width)
 
     lines = jnp.arange(chips * cap, dtype=jnp.int32)
@@ -93,7 +97,8 @@
             "td,hd->th", tokens, down_part, preferred_element_type=jnp.float32
         ).astype(jnp.bfloat16)
 
-    hidden_grad = jnp.stack([hidden(from_next), hidden(from_prev)])
+    next_tokens, _ = lax.optimization_barrier((from_next, packed))
+    hidden_grad = jnp.stack([hidden(next_tokens), hidden(from_prev)])
     return (
         sent.reshape(1, 1, 1, buffer_rows, width),
         section_grad[None],

time: 111 us -> 107 us (0.964)
  starting transfers between devices: 50.4 us -> 45.9 us
  waiting for transfers between devices: 41.5 us -> 43.4 us
    ppermute x2, waiting for transfers between devices: 18.1 us -> 0.01 us  [shifted(): return lax.ppermute(array, axis, pairs)]
    all_to_all x2, waiting for transfers between devices: 22 us -> 32.5 us  [exchanged(): lax.all_to_all(pieces, 'expert', split_axis=0, concat_axis=0, tiled=True,...]
    ppermute x5, waiting for transfers between devices: 1.42 us -> 10.9 us  [swapped(): return lax.ppermute(array, axis, [(i, i ^ 1) for i in range(peers)])]
    all_to_all x2, starting transfers between devices: 30.5 us -> 26.4 us  [exchanged(): lax.all_to_all(pieces, 'expert', split_axis=0, concat_axis=0, tiled=True,...]
    squeeze x1, local copies, waits for them, and re-layouts: 0.06 us -> 1.28 us  [on_device(): pieces, own_a = lax.optimization_barrier((pieces, grad_in[0, 0]))]
  transfers between devices with their start and end apart: 9 -> 9, of which waited for: 5 -> 3; matrix products, arithmetic and copies ran while one was open for 13% -> 11% of each run, Pallas kernels for 0% -> 0%
where the time goes in v2:
time: 107 us; the launch traced here: 106 us
  starting transfers between devices  45.9 us (43%)
  waiting for transfers between devices  43.4 us (41%)
  matrix products  7.71 us (7%)
  local copies, waits for them, and re-layouts  5.58 us (5%)
  other arithmetic  2.68 us (3%)
    all_to_all x2, waiting for transfers between devices, exchanged(): lax.all_to_all(pieces, 'expert', split_axis=0, concat_axis=0, tiled=True,...  32.5 us
    all_to_all x2, starting transfers between devices, exchanged(): lax.all_to_all(pieces, 'expert', split_axis=0, concat_axis=0, tiled=True,...  26.4 us
    ppermute x5, starting transfers between devices, swapped(): return lax.ppermute(array, axis, [(i, i ^ 1) for i in range(peers)])  11.9 us
    ppermute x5, waiting for transfers between devices, swapped(): return lax.ppermute(array, axis, [(i, i ^ 1) for i in range(peers)])  10.9 us
    ppermute x2, starting transfers between devices, shifted(): return lax.ppermute(array, axis, pairs)  7.63 us
    dot_general x2, matrix products, hidden(): jnp.einsum('td,hd->th', tokens, down_part, preferred_element_type=jnp.flo...  4.63 us
  transfers between devices with their start and end apart: 9, of which 3 were waited for; matrix products, arithmetic and copies ran while one was open for 11% of the time, Pallas kernels for 0%

profile of v2, /device:TPU:56, one launch (start us, length us, event | category | flops | bytes accessed | tf_op | source)
XLA Modules:
  0.0 106.1 jit_solution(15532733572243854746)
XLA Ops:
  0.6 0.0 copy-start
  0.6 1.3 %slice_bitcast_fusion = (bf16[64,3584]{1,0:T(8,128)(2,1)S(1)}, bf16[64,3584]{1,0:T(8,128)(2,1)S(1)}) fusion(bf16[2,1,64,3584]{3,2,1,0:T(8,128)(2,1)} %param.5), kind=kLoop, calls=%fused_computation.23 | loop fusion | bytes 1835008 | tf_op jit(solution)/shard_map/squeeze | solution.py:50
  1.9 0.1 copy-done
  2.0 0.0 copy-start.1
  2.0 0.0 copy-start.2
  2.0 1.3 %reshape_squeeze.3 = bf16[16,24,896]{2,1,0:T(8,128)(2,1)} reshape(bf16[1,1,1,96,3584]{4,3,2,1,0:T(8,128)(2,1)S(1)} %copy-done) | data formatting | bytes 1376256 | tf_op jit(solution)/shard_map/reshape;squeeze | solution.py:49
  3.3 5.7 %collective-permute-start = (bf16[64,3584]{1,0:T(8,128)(2,1)S(1)}, bf16[64,3584]{1,0:T(8,128)(2,1)S(1)}, u32[]{:S(2)}, u32[]{:S(2)}) collective-permute-start(bf16[64,3584]{1,0:T(8,128)(2,1)S(1)} %get-tuple-element.11), channel_id=1, source_target_pairs={{64,0},{128,64},{192,128},{256,192},{320,256},{384,320},{448,384},... | collective-permute-start | bytes 1376264 | tf_op jit(solution)/shard_map/ppermute | solution.py:13
  9.0 18.9 %all-to-all-start.1 = ((bf16[16,24,896]{2,1,0:T(8,128)(2,1)}), bf16[16,24,896]{2,1,0:T(8,128)(2,1)S(1)}, u32[]{:S(2)}, u32[]{:S(2)}) async-start(bf16[16,24,896]{2,1,0:T(8,128)(2,1)} %reshape_squeeze.3), calls=%async_computation.1 | async-start | bytes 1376256 | tf_op jit(solution)/shard_map/all_to_all | solution.py:45
  27.9 0.0 copy-done.1
  27.9 0.2 convert_reduce_fusion
  28.1 0.2 convert_reduce_fusion.2
  28.3 0.0 collective-permute-done
  28.3 0.0 copy-done.2
  28.3 0.1 multiply_convert_fusion
  28.5 1.9 %collective-permute-start.2 = (bf16[64,3584]{1,0:T(8,128)(2,1)S(1)}, bf16[64,3584]{1,0:T(8,128)(2,1)}, u32[]{:S(2)}, u32[]{:S(2)}) collective-permute-start(bf16[64,3584]{1,0:T(8,128)(2,1)S(1)} %multiply_convert_fusion), channel_id=1, source_target_pairs={{0,2},{2,0},{4,6},{6,4},{8,10},{10,8},{12,14},{14,12},{16,18},{18,... | collective-permute-start | bytes 1376264 | tf_op jit(solution)/shard_map/ppermute | solution.py:18
  30.4 2.4 %collective-permute-start.1 = (s32[64]{0:T(128)S(1)}, s32[64]{0:T(128)S(1)}, u32[]{:S(2)}, u32[]{:S(2)}) collective-permute-start(s32[64]{0:T(128)S(1)} %get-tuple-element.12), channel_id=1, source_target_pairs={{0,2},{2,0},{4,6},{6,4},{8,10},{10,8},{12,14},{14,12},{16,18},{18,... | collective-permute-start | bytes 776 | tf_op jit(solution)/shard_map/ppermute | solution.py:18
  32.8 1.9 %collective-permute-start.3 = (bf16[64,3584]{1,0:T(8,128)(2,1)S(1)}, bf16[64,3584]{1,0:T(8,128)(2,1)S(1)}, u32[]{:S(2)}, u32[]{:S(2)}) collective-permute-start(bf16[64,3584]{1,0:T(8,128)(2,1)S(1)} %get-tuple-element.14), channel_id=1, source_target_pairs={{0,64},{64,128},{128,192},{192,256},{256,320},{320,384},{384,448},... | collective-permute-start | bytes 1376264 | tf_op jit(solution)/shard_map/ppermute | solution.py:13
  34.8 0.0 collective-permute-done.1
  34.8 0.2 convert_reduce_fusion.1
  35.0 0.1 pad_add_fusion
  35.1 0.0 collective-permute-done.2
  35.1 1.4 %convolution_convert_fusion = bf16[96,3584]{1,0:T(8,128)(2,1)S(1)} fusion(bf16[64,3584]{1,0:T(8,128)(2,1)} %collective-permute-done.2, bf16[64,3584]{1,0:T(8,128)(2,1)S(1)} %multiply_convert_fusion, s32[128]{0:T(128)S(1)} %pad_add_fusion), kind=kOutput, calls=%fused_computation | convolution fusion | flops 90271744 | bytes 1606144 | tf_op jit(solution)/shard_map/dot_general | solution.py:71
  36.4 3.1 %collective-permute-start.5 = (bf16[64,3584]{1,0:T(8,128)(2,1)S(1)}, bf16[64,3584]{1,0:T(8,128)(2,1)}, u32[]{:S(2)}, u32[]{:S(2)}) collective-permute-start(bf16[64,3584]{1,0:T(8,128)(2,1)S(1)} %collective-permute-done), channel_id=1, source_target_pairs={{0,1},{1,0},{2,3},{3,2},{4,5},{5,4},{6,7},{7,6},{8,9},{9,8},{10,11... | collective-permute-start | bytes 1376264 | tf_op jit(solution)/shard_map/ppermute | solution.py:18
  39.6 1.3 %reshape.115 = bf16[16,24,896]{2,1,0:T(8,128)(2,1)} reshape(bf16[96,3584]{1,0:T(8,128)(2,1)S(1)} %convolution_convert_fusion) | data formatting | bytes 1376256 | tf_op jit(solution)/shard_map/reshape | solution.py:73
  40.8 21.7 %all-to-all-done.1 = bf16[16,24,896]{2,1,0:T(8,128)(2,1)S(1)} async-done(((bf16[16,24,896]{2,1,0:T(8,128)(2,1)}), bf16[16,24,896]{2,1,0:T(8,128)(2,1)S(1)}, u32[]{:S(2)}, u32[]{:S(2)}) %all-to-all-start.1) | async-done | bytes 688160 | tf_op jit(solution)/shard_map/all_to_all | solution.py:45
  62.5 7.5 %all-to-all-start = ((bf16[16,24,896]{2,1,0:T(8,128)(2,1)}), bf16[16,24,896]{2,1,0:T(8,128)(2,1)S(1)}, u32[]{:S(2)}, u32[]{:S(2)}) async-start(bf16[16,24,896]{2,1,0:T(8,128)(2,1)} %reshape.115), calls=%async_computation | async-start | bytes 1376256 | tf_op jit(solution)/shard_map/all_to_all | solution.py:45
  70.0 0.4 reshape.116
  70.4 0.0 collective-permute-done.3
  70.4 0.3 convolution_convert_fusion.1
  70.7 1.9 %collective-permute-start.4 = (bf16[48,3584]{1,0:T(8,128)(2,1)S(1)}, bf16[48,3584]{1,0:T(8,128)(2,1)S(1)}, u32[]{:S(2)}, u32[]{:S(2)}) collective-permute-start(bf16[48,3584]{1,0:T(8,128)(2,1)S(1)} %convolution_convert_fusion.1), channel_id=1, source_target_pairs={{0,2},{2,0},{4,6},{6,4},{8,10},{10,8},{12,14},{14,12},{16,18},{18,... | collective-permute-start | bytes 1032200 | tf_op jit(solution)/shard_map/ppermute | solution.py:18
  72.7 0.0 collective-permute-done.5
  72.7 1.1 %broadcast_select_fusion.3 = (bf16[64,3584]{1,0:T(8,128)(2,1)S(1)}, bf16[64,3584]{1,0:T(8,128)(2,1)S(1)}) fusion(bf16[64,3584]{1,0:T(8,128)(2,1)S(1)} %collective-permute-done, bf16[64,3584]{1,0:T(8,128)(2,1)} %collective-permute-done.5, pred[]{:T(512)S(6)} %eq.151), kind=kLoop, calls=%fused_computation.28 | loop fusion | flops 458752 | bytes 1835009 | tf_op jit(solution)/shard_map/jit(_where)/select_n | solution.py:93
  73.8 3.3 %fusion.13 = bf16[1,128,512]{2,1,0:T(8,128)(2,1)S(1)} fusion(bf16[1,512,3584]{2,1,0:T(8,128)(2,1)} %param.9, bf16[64,3584]{1,0:T(8,128)(2,1)S(1)} %get-tuple-element.29, bf16[64,3584]{1,0:T(8,128)(2,1)S(1)} %get-tuple-element.28), kind=kOutput, calls=%fused_computation.10 | convolution fusion | flops 471662592 | bytes 4718592 | tf_op jit(solution)/shard_map/td,hd->th/dot_general | solution.py:96
  77.1 2.5 %collective-permute-start.6 = (bf16[64,3584]{1,0:T(8,128)(2,1)S(1)}, bf16[64,3584]{1,0:T(8,128)(2,1)S(1)}, u32[]{:S(2)}, u32[]{:S(2)}) collective-permute-start(bf16[64,3584]{1,0:T(8,128)(2,1)S(1)} %collective-permute-done.3), channel_id=1, source_target_pairs={{0,1},{1,0},{2,3},{3,2},{4,5},{5,4},{6,7},{7,6},{8,9},{9,8},{10,11... | collective-permute-start | bytes 1376264 | tf_op jit(solution)/shard_map/ppermute | solution.py:18
  79.6 0.0 collective-permute-done.4
  79.6 0.3 fusion.29
  80.0 0.0 copy-start.3
  80.0 1.1 %fusion.25 = bf16[1,64,3584]{2,1,0:T(8,128)(2,1)} fusion(bf16[64,3584]{1,0:T(8,128)(2,1)S(1)} %collective-permute-done.3, f32[64,3584]{1,0:T(8,128)S(1)} %fusion.29, bf16[96,3584]{1,0:T(8,128)(2,1)S(1)} %reshape.116, s32[64]{0:T(128)S(1)} %get-tuple-element.25), kind=kOutput, calls=%fused_computation.22 | convolution fusion | flops 44963840 | bytes 2523392 | tf_op jit(solution)/shard_map/dot_general | solution.py:83
  81.1 10.8 %collective-permute-done.6 = bf16[64,3584]{1,0:T(8,128)(2,1)S(1)} collective-permute-done((bf16[64,3584]{1,0:T(8,128)(2,1)S(1)}, bf16[64,3584]{1,0:T(8,128)(2,1)S(1)}, u32[]{:S(2)}, u32[]{:S(2)}) %collective-permute-start.6) | collective-permute-done | bytes 458784 | tf_op jit(solution)/shard_map/ppermute | solution.py:18
  91.9 0.1 broadcast_select_fusion.1
  92.0 0.0 copy-done.3
  92.0 1.3 %fusion.10 = bf16[1,128,512]{2,1,0:T(8,128)(2,1)S(1)} fusion(bf16[1,512,3584]{2,1,0:T(8,128)(2,1)S(1)} %copy-done.3, bf16[64,3584]{1,0:T(8,128)(2,1)S(1)} %get-tuple-element.31, bf16[64,3584]{1,0:T(8,128)(2,1)S(1)} %get-tuple-element.30), kind=kOutput, calls=%fused_computation.9 | convolution fusion | flops 471662592 | bytes 4718592 | tf_op jit(solution)/shard_map/td,hd->th/dot_general | solution.py:96
  93.3 0.7 maximum_bitcast_fusion
  94.0 10.8 %all-to-all-done = bf16[16,24,896]{2,1,0:T(8,128)(2,1)S(1)} async-done(((bf16[16,24,896]{2,1,0:T(8,128)(2,1)}), bf16[16,24,896]{2,1,0:T(8,128)(2,1)S(1)}, u32[]{:S(2)}, u32[]{:S(2)}) %all-to-all-start) | async-done | bytes 688160 | tf_op jit(solution)/shard_map/all_to_all | solution.py:45
  104.8 1.3 %reshape_reshape.3 = bf16[1,1,1,96,3584]{4,3,2,1,0:T(8,128)(2,1)} reshape(bf16[16,24,896]{2,1,0:T(8,128)(2,1)S(1)} %all-to-all-done) | data formatting | bytes 1376256 | tf_op jit(solution)/shard_map/reshape;reshape | solution.py:103
  (5 shorter events, 0.1 us)
Async XLA Ops:
  0.6 1.4 %copy-start = (bf16[1,1,1,96,3584]{4,3,2,1,0:T(8,128)(2,1)S(1)}, bf16[1,1,1,96,3584]{4,3,2,1,0:T(8,128)(2,1)}, u32[]{:S(2)}) copy-start(bf16[1,1,1,96,3584]{4,3,2,1,0:T(8,128)(2,1)} %param.8) | copy-start | bytes 2064388
  2.0 25.9 %copy-start.1 = (s32[2,1,64,1]{2,3,1,0:T(1,128)S(1)}, s32[2,1,64,1]{2,3,1,0:T(1,128)}, u32[]{:S(2)}) copy-start(s32[2,1,64,1]{2,3,1,0:T(1,128)} %param.6) | copy-start | bytes 1540
  2.0 26.3 %copy-start.2 = (f32[1,64]{1,0:T(1,128)S(1)}, f32[1,64]{1,0:T(1,128)}, u32[]{:S(2)}) copy-start(f32[1,64]{1,0:T(1,128)} %param.7) | copy-start | bytes 772
  3.3 25.0 %collective-permute-start = (bf16[64,3584]{1,0:T(8,128)(2,1)S(1)}, bf16[64,3584]{1,0:T(8,128)(2,1)S(1)}, u32[]{:S(2)}, u32[]{:S(2)}) collective-permute-start(bf16[64,3584]{1,0:T(8,128)(2,1)S(1)} %get-tuple-element.11), channel_id=1, source_target_pairs={{64,0},{128,64},{192,128},{256,192},{320,256},{384,320},{448,384},... | collective-permute-start | bytes 1376264 | tf_op jit(solution)/shard_map/ppermute | solution.py:13
  9.0 53.5 %all-to-all-start.1 = ((bf16[16,24,896]{2,1,0:T(8,128)(2,1)}), bf16[16,24,896]{2,1,0:T(8,128)(2,1)S(1)}, u32[]{:S(2)}, u32[]{:S(2)}) async-start(bf16[16,24,896]{2,1,0:T(8,128)(2,1)} %reshape_squeeze.3), calls=%async_computation.1 | async-start | bytes 1376256 | tf_op jit(solution)/shard_map/all_to_all | solution.py:45
  28.5 6.6 %collective-permute-start.2 = (bf16[64,3584]{1,0:T(8,128)(2,1)S(1)}, bf16[64,3584]{1,0:T(8,128)(2,1)}, u32[]{:S(2)}, u32[]{:S(2)}) collective-permute-start(bf16[64,3584]{1,0:T(8,128)(2,1)S(1)} %multiply_convert_fusion), channel_id=1, source_target_pairs={{0,2},{2,0},{4,6},{6,4},{8,10},{10,8},{12,14},{14,12},{16,18},{18,... | collective-permute-start | bytes 1376264 | tf_op jit(solution)/shard_map/ppermute | solution.py:18
  30.4 4.4 %collective-permute-start.1 = (s32[64]{0:T(128)S(1)}, s32[64]{0:T(128)S(1)}, u32[]{:S(2)}, u32[]{:S(2)}) collective-permute-start(s32[64]{0:T(128)S(1)} %get-tuple-element.12), channel_id=1, source_target_pairs={{0,2},{2,0},{4,6},{6,4},{8,10},{10,8},{12,14},{14,12},{16,18},{18,... | collective-permute-start | bytes 776 | tf_op jit(solution)/shard_map/ppermute | solution.py:18
  32.8 37.6 %collective-permute-start.3 = (bf16[64,3584]{1,0:T(8,128)(2,1)S(1)}, bf16[64,3584]{1,0:T(8,128)(2,1)S(1)}, u32[]{:S(2)}, u32[]{:S(2)}) collective-permute-start(bf16[64,3584]{1,0:T(8,128)(2,1)S(1)} %get-tuple-element.14), channel_id=1, source_target_pairs={{0,64},{64,128},{128,192},{192,256},{256,320},{320,384},{384,448},... | collective-permute-start | bytes 1376264 | tf_op jit(solution)/shard_map/ppermute | solution.py:13
  36.4 36.3 %collective-permute-start.5 = (bf16[64,3584]{1,0:T(8,128)(2,1)S(1)}, bf16[64,3584]{1,0:T(8,128)(2,1)}, u32[]{:S(2)}, u32[]{:S(2)}) collective-permute-start(bf16[64,3584]{1,0:T(8,128)(2,1)S(1)} %collective-permute-done), channel_id=1, source_target_pairs={{0,1},{1,0},{2,3},{3,2},{4,5},{5,4},{6,7},{7,6},{8,9},{9,8},{10,11... | collective-permute-start | bytes 1376264 | tf_op jit(solution)/shard_map/ppermute | solution.py:18
  62.5 42.3 %all-to-all-start = ((bf16[16,24,896]{2,1,0:T(8,128)(2,1)}), bf16[16,24,896]{2,1,0:T(8,128)(2,1)S(1)}, u32[]{:S(2)}, u32[]{:S(2)}) async-start(bf16[16,24,896]{2,1,0:T(8,128)(2,1)} %reshape.115), calls=%async_computation | async-start | bytes 1376256 | tf_op jit(solution)/shard_map/all_to_all | solution.py:45
  70.7 8.9 %collective-permute-start.4 = (bf16[48,3584]{1,0:T(8,128)(2,1)S(1)}, bf16[48,3584]{1,0:T(8,128)(2,1)S(1)}, u32[]{:S(2)}, u32[]{:S(2)}) collective-permute-start(bf16[48,3584]{1,0:T(8,128)(2,1)S(1)} %convolution_convert_fusion.1), channel_id=1, source_target_pairs={{0,2},{2,0},{4,6},{6,4},{8,10},{10,8},{12,14},{14,12},{16,18},{18,... | collective-permute-start | bytes 1032200 | tf_op jit(solution)/shard_map/ppermute | solution.py:18
  77.1 14.8 %collective-permute-start.6 = (bf16[64,3584]{1,0:T(8,128)(2,1)S(1)}, bf16[64,3584]{1,0:T(8,128)(2,1)S(1)}, u32[]{:S(2)}, u32[]{:S(2)}) collective-permute-start(bf16[64,3584]{1,0:T(8,128)(2,1)S(1)} %collective-permute-done.3), channel_id=1, source_target_pairs={{0,1},{1,0},{2,3},{3,2},{4,5},{5,4},{6,7},{7,6},{8,9},{9,8},{10,11... | collective-permute-start | bytes 1376264 | tf_op jit(solution)/shard_map/ppermute | solution.py:18
  80.0 12.0 %copy-start.3 = (bf16[1,512,3584]{2,1,0:T(8,128)(2,1)S(1)}, bf16[1,512,3584]{2,1,0:T(8,128)(2,1)}, u32[]{:S(2)}) copy-start(bf16[1,512,3584]{2,1,0:T(8,128)(2,1)} %param.9) | copy-start | bytes 11010052

commit v3 on v2

--- a/solution.py
+++ b/solution.py
@@ -47,30 +47,38 @@
         )
 
     pieces = back_rows[0, 0, 0].reshape(chips, chip_rows * PARTS, part)
-    pieces, own_a = lax.optimization_barrier((pieces, grad_in[0, 0]))
+    pieces, grads = lax.optimization_barrier((pieces, grad_in))
+    own_a = grads[0, 0]
     came = exchanged(pieces)
     came = came.reshape(buffer_rows, width)
 
     from_next = shifted(own_a, "section", -1)
     ident_a = expert_ids[0, 0, :, 0]
     ident_b = expert_ids[1, 0, :, 0]
-    own_ident, own_b, from_next = lax.optimization_barrier((ident_a, grad_in[1, 0], from_next))
+    own_b, from_next = lax.optimization_barrier((grads[1, 0], from_next))
     from_prev = shifted(own_b, "section", 1)
-    ident_mate = swapped(own_ident, "expert")
 
+    tokens = ident_a.shape[0]
+    row_a = (ident_a // CORES) * chip_rows + core * cap + slot_of(ident_a)
+    here = ident_a % CORES == core
+    numbers = jnp.where(here, buffer_rows, row_a).astype(jnp.bfloat16)[None, :]
+    numbers = jnp.pad(numbers, ((0, 7), (0, width - tokens)))
     scaled = (gate_weights[0][:, None] * from_next.astype(jnp.float32)).astype(jnp.bfloat16)
-    scaled_mate = swapped(scaled, "expert")
-    chip_tokens = jnp.concatenate([scaled, scaled_mate], axis=0)
-
-    def place(ident, source):
-        row = (ident // CORES) * chip_rows + source * cap + slot_of(ident)
-        return jnp.where(ident % CORES == core, row, buffer_rows)
-
-    target = jnp.concatenate([place(ident_a, core), place(ident_mate, other)])
-    table = (jnp.arange(buffer_rows, dtype=jnp.int32)[:, None] == target[None, :]).astype(jnp.bfloat16)
-    packed = jnp.dot(table, chip_tokens, preferred_element_type=jnp.float32).astype(jnp.bfloat16)
+    mate = swapped(jnp.concatenate([scaled, numbers], axis=0), "expert")
+    target = jnp.concatenate(
+        [jnp.where(here, row_a, buffer_rows), mate[tokens, :tokens].astype(jnp.int32)]
+    )
+    spread = jnp.concatenate(
+        [array[:tokens, g * part : (g + 1) * part] for g in range(PARTS) for array in (scaled, mate)],
+        axis=0,
+    )
+    target = jnp.concatenate([target * PARTS + g for g in range(PARTS)])
+    line = jnp.arange(buffer_rows * PARTS, dtype=jnp.int32)
+    table = (line[:, None] == target[None, :]).astype(jnp.bfloat16)
+    packed = jnp.dot(table, spread, preferred_element_type=jnp.float32).astype(jnp.bfloat16)
+    packed = packed.reshape(chips, chip_rows * PARTS, part)
+    sent = exchanged(packed).reshape(buffer_rows, width)
     from_prev, came = lax.optimization_barrier((from_prev, came))
-    sent = exchanged(packed.reshape(chips, chip_rows * PARTS, part)).reshape(buffer_rows, width)
 
     lines = jnp.arange(chips * cap, dtype=jnp.int32)
     passed = select((lines // cap) * chip_rows + other * cap + lines % cap, buffer_rows)

time: 107 us -> 101 us (0.944)
  waiting for transfers between devices: 43.4 us -> 39.1 us
  starting transfers between devices: 45.9 us -> 44.8 us
    all_to_all x2, waiting for transfers between devices: 32.5 us -> 19.9 us  [exchanged(): lax.all_to_all(pieces, 'expert', split_axis=0, concat_axis=0, tiled=True,...]
    ppermute x2, waiting for transfers between devices: 0.01 us -> 9.23 us  [shifted(): return lax.ppermute(array, axis, pairs)]
    reshape x1 -> x0, local copies, waits for them, and re-layouts: 1.26 us -> none  [on_device(): packed.reshape(chips, chip_rows * PARTS, part)]
    ppermute x5 -> x4, starting transfers between devices: 11.9 us -> 10.9 us  [swapped(): return lax.ppermute(array, axis, [(i, i ^ 1) for i in range(peers)])]
    ppermute x5 -> x4, waiting for transfers between devices: 10.9 us -> 9.97 us  [swapped(): return lax.ppermute(array, axis, [(i, i ^ 1) for i in range(peers)])]
  transfers between devices with their start and end apart: 9 -> 8, of which waited for: 3 -> 4; matrix products, arithmetic and copies ran while one was open for 11% -> 12% of each run, Pallas kernels for 0% -> 0%
where the time goes in v3:
time: 101 us; the launch traced here: 100 us
  starting transfers between devices  44.8 us (44%)
  waiting for transfers between devices  39.1 us (39%)
  matrix products  7.77 us (8%)
  local copies, waits for them, and re-layouts  5.31 us (5%)
  other arithmetic  2.57 us (3%)
    all_to_all x2, starting transfers between devices, exchanged(): lax.all_to_all(pieces, 'expert', split_axis=0, concat_axis=0, tiled=True,...  26.3 us
    all_to_all x2, waiting for transfers between devices, exchanged(): lax.all_to_all(pieces, 'expert', split_axis=0, concat_axis=0, tiled=True,...  19.9 us
    ppermute x4, starting transfers between devices, swapped(): return lax.ppermute(array, axis, [(i, i ^ 1) for i in range(peers)])  10.9 us
    ppermute x4, waiting for transfers between devices, swapped(): return lax.ppermute(array, axis, [(i, i ^ 1) for i in range(peers)])  9.97 us
    ppermute x2, waiting for transfers between devices, shifted(): return lax.ppermute(array, axis, pairs)  9.23 us
    ppermute x2, starting transfers between devices, shifted(): return lax.ppermute(array, axis, pairs)  7.64 us
    dot_general x2, matrix products, hidden(): jnp.einsum('td,hd->th', tokens, down_part, preferred_element_type=jnp.flo...  4.63 us
    another operation x1, local copies, waits for them, and re-layouts, on_device(): pieces = back_rows[0, 0, 0].reshape(chips, chip_rows * PARTS, part)  2.28 us
  transfers between devices with their start and end apart: 8, of which 4 were waited for; matrix products, arithmetic and copies ran while one was open for 12% of the time, Pallas kernels for 0%

profile of v3, /device:TPU:56, one launch (start us, length us, event | category | flops | bytes accessed | tf_op | source)
XLA Modules:
  0.0 100.5 jit_solution(3874194846149497830)
XLA Ops:
  0.6 0.0 copy-start
  0.6 0.0 copy-start.1
  0.7 2.3 %reshape_squeeze.3 = bf16[16,24,896]{2,1,0:T(8,128)(2,1)} reshape(bf16[1,1,1,96,3584]{4,3,2,1,0:T(8,128)(2,1)} %param.8) | data formatting | bytes 1376256 | tf_op jit(solution)/shard_map/reshape;squeeze | solution.py:49
  2.9 18.9 %all-to-all-start.1 = ((bf16[16,24,896]{2,1,0:T(8,128)(2,1)}), bf16[16,24,896]{2,1,0:T(8,128)(2,1)S(1)}, u32[]{:S(2)}, u32[]{:S(2)}) async-start(bf16[16,24,896]{2,1,0:T(8,128)(2,1)} %reshape_squeeze.3), calls=%async_computation.1 | async-start | bytes 1376256 | tf_op jit(solution)/shard_map/all_to_all | solution.py:45
  21.8 1.2 %slice_bitcast_fusion = (bf16[64,3584]{1,0:T(8,128)(2,1)S(1)}, bf16[64,3584]{1,0:T(8,128)(2,1)S(1)}) fusion(bf16[2,1,64,3584]{3,2,1,0:T(8,128)(2,1)} %param.5), kind=kLoop, calls=%fused_computation.24 | loop fusion | bytes 1835008 | tf_op jit(solution)/shard_map/squeeze | solution.py:51
  23.0 5.7 %collective-permute-start = (bf16[64,3584]{1,0:T(8,128)(2,1)S(1)}, bf16[64,3584]{1,0:T(8,128)(2,1)S(1)}, u32[]{:S(2)}, u32[]{:S(2)}) collective-permute-start(bf16[64,3584]{1,0:T(8,128)(2,1)S(1)} %get-tuple-element.32), channel_id=1, source_target_pairs={{64,0},{128,64},{192,128},{256,192},{320,256},{384,320},{448,384},... | collective-permute-start | bytes 1376264 | tf_op jit(solution)/shard_map/ppermute | solution.py:13
  28.7 0.0 copy-done
  28.8 0.2 convert_reduce_fusion
  29.0 0.2 convert_reduce_fusion.1
  29.2 9.2 %collective-permute-done = bf16[64,3584]{1,0:T(8,128)(2,1)S(1)} collective-permute-done((bf16[64,3584]{1,0:T(8,128)(2,1)S(1)}, bf16[64,3584]{1,0:T(8,128)(2,1)S(1)}, u32[]{:S(2)}, u32[]{:S(2)}) %collective-permute-start) | collective-permute-done | bytes 458784 | tf_op jit(solution)/shard_map/ppermute | solution.py:13
  38.4 0.0 copy-done.1
  38.4 0.1 multiply_convert_fusion
  38.6 1.9 %collective-permute-start.1 = (bf16[72,3584]{1,0:T(8,128)(2,1)S(1)}, bf16[72,3584]{1,0:T(8,128)(2,1)S(1)}, u32[]{:S(2)}, u32[]{:S(2)}) collective-permute-start(bf16[72,3584]{1,0:T(8,128)(2,1)S(1)} %fusion.23), channel_id=1, source_target_pairs={{0,2},{2,0},{4,6},{6,4},{8,10},{10,8},{12,14},{14,12},{16,18},{18,... | collective-permute-start | bytes 1548296 | tf_op jit(solution)/shard_map/ppermute | solution.py:18
  40.6 1.9 %collective-permute-start.2 = (bf16[64,3584]{1,0:T(8,128)(2,1)S(1)}, bf16[64,3584]{1,0:T(8,128)(2,1)S(1)}, u32[]{:S(2)}, u32[]{:S(2)}) collective-permute-start(bf16[64,3584]{1,0:T(8,128)(2,1)S(1)} %get-tuple-element.12), channel_id=1, source_target_pairs={{0,64},{64,128},{128,192},{192,256},{256,320},{320,384},{384,448},... | collective-permute-start | bytes 1376264 | tf_op jit(solution)/shard_map/ppermute | solution.py:13
  42.5 0.0 collective-permute-done.1
  42.5 0.1 broadcast_add_fusion.2
  42.8 1.4 %convolution_convert_fusion.1 = bf16[384,896]{1,0:T(8,128)(2,1)} fusion(bf16[512,896]{1,0:T(8,128)(2,1)S(1)} %slice_dynamic-update-slice_fusion, s32[512]{0:T(512)S(1)} %pad_add_fusion), kind=kOutput, calls=%fused_computation.6 | convolution fusion | flops 352862208 | bytes 1607680 | tf_op jit(solution)/shard_map/dot_general | solution.py:78
  44.2 3.4 %collective-permute-start.4 = (bf16[64,3584]{1,0:T(8,128)(2,1)S(1)}, bf16[64,3584]{1,0:T(8,128)(2,1)}, u32[]{:S(2)}, u32[]{:S(2)}) collective-permute-start(bf16[64,3584]{1,0:T(8,128)(2,1)S(1)} %collective-permute-done), channel_id=1, source_target_pairs={{0,1},{1,0},{2,3},{3,2},{4,5},{5,4},{6,7},{7,6},{8,9},{9,8},{10,11... | collective-permute-start | bytes 1376264 | tf_op jit(solution)/shard_map/ppermute | solution.py:18
  47.6 9.1 %all-to-all-done.1 = bf16[16,24,896]{2,1,0:T(8,128)(2,1)S(1)} async-done(((bf16[16,24,896]{2,1,0:T(8,128)(2,1)}), bf16[16,24,896]{2,1,0:T(8,128)(2,1)S(1)}, u32[]{:S(2)}, u32[]{:S(2)}) %all-to-all-start.1) | async-done | bytes 688160 | tf_op jit(solution)/shard_map/all_to_all | solution.py:45
  56.8 7.4 %all-to-all-start = ((bf16[16,24,896]{2,1,0:T(8,128)(2,1)}), bf16[16,24,896]{2,1,0:T(8,128)(2,1)S(1)}, u32[]{:S(2)}, u32[]{:S(2)}) async-start(bf16[16,24,896]{2,1,0:T(8,128)(2,1)} %bitcast.7), calls=%async_computation | async-start | bytes 1376256 | tf_op jit(solution)/shard_map/all_to_all | solution.py:45
  64.2 0.4 reshape.233
  64.6 0.0 collective-permute-done.2
  64.6 0.3 convolution_convert_fusion
  64.9 1.9 %collective-permute-start.3 = (bf16[48,3584]{1,0:T(8,128)(2,1)S(1)}, bf16[48,3584]{1,0:T(8,128)(2,1)S(1)}, u32[]{:S(2)}, u32[]{:S(2)}) collective-permute-start(bf16[48,3584]{1,0:T(8,128)(2,1)S(1)} %convolution_convert_fusion), channel_id=1, source_target_pairs={{0,2},{2,0},{4,6},{6,4},{8,10},{10,8},{12,14},{14,12},{16,18},{18,... | collective-permute-start | bytes 1032200 | tf_op jit(solution)/shard_map/ppermute | solution.py:18
  66.9 0.0 collective-permute-done.4
  66.9 1.1 %broadcast_select_fusion.3 = (bf16[64,3584]{1,0:T(8,128)(2,1)S(1)}, bf16[64,3584]{1,0:T(8,128)(2,1)S(1)}) fusion(bf16[64,3584]{1,0:T(8,128)(2,1)S(1)} %collective-permute-done, bf16[64,3584]{1,0:T(8,128)(2,1)} %collective-permute-done.4, pred[]{:T(512)S(6)} %eq.142), kind=kLoop, calls=%fused_computation.29 | loop fusion | flops 458752 | bytes 1835009 | tf_op jit(solution)/shard_map/jit(_where)/select_n | solution.py:101
  68.0 3.3 %fusion.13 = bf16[1,128,512]{2,1,0:T(8,128)(2,1)S(1)} fusion(bf16[1,512,3584]{2,1,0:T(8,128)(2,1)} %param.9, bf16[64,3584]{1,0:T(8,128)(2,1)S(1)} %get-tuple-element.29, bf16[64,3584]{1,0:T(8,128)(2,1)S(1)} %get-tuple-element.28), kind=kOutput, calls=%fused_computation.10 | convolution fusion | flops 471662592 | bytes 4718592 | tf_op jit(solution)/shard_map/td,hd->th/dot_general | solution.py:104
  71.3 0.0 copy-start.2
  71.3 3.7 %collective-permute-start.5 = (bf16[64,3584]{1,0:T(8,128)(2,1)S(1)}, bf16[64,3584]{1,0:T(8,128)(2,1)S(1)}, u32[]{:S(2)}, u32[]{:S(2)}) collective-permute-start(bf16[64,3584]{1,0:T(8,128)(2,1)S(1)} %collective-permute-done.2), channel_id=1, source_target_pairs={{0,1},{1,0},{2,3},{3,2},{4,5},{5,4},{6,7},{7,6},{8,9},{9,8},{10,11... | collective-permute-start | bytes 1376264 | tf_op jit(solution)/shard_map/ppermute | solution.py:18
  75.0 0.0 collective-permute-done.3
  75.0 0.3 fusion.28
  75.3 1.1 %fusion.24 = bf16[1,64,3584]{2,1,0:T(8,128)(2,1)} fusion(bf16[64,3584]{1,0:T(8,128)(2,1)S(1)} %collective-permute-done.2, f32[64,3584]{1,0:T(8,128)S(1)} %fusion.28, bf16[96,3584]{1,0:T(8,128)(2,1)S(1)} %reshape.233, s32[64]{0:T(128)S(1)} %get-tuple-element.23), kind=kOutput, calls=%fused_computation.23 | convolution fusion | flops 44963840 | bytes 2523392 | tf_op jit(solution)/shard_map/dot_general | solution.py:91
  76.4 10.0 %collective-permute-done.5 = bf16[64,3584]{1,0:T(8,128)(2,1)S(1)} collective-permute-done((bf16[64,3584]{1,0:T(8,128)(2,1)S(1)}, bf16[64,3584]{1,0:T(8,128)(2,1)S(1)}, u32[]{:S(2)}, u32[]{:S(2)}) %collective-permute-start.5) | collective-permute-done | bytes 458784 | tf_op jit(solution)/shard_map/ppermute | solution.py:18
  86.4 0.1 broadcast_select_fusion.1
  86.5 0.0 copy-done.2
  86.5 1.3 %fusion.10 = bf16[1,128,512]{2,1,0:T(8,128)(2,1)S(1)} fusion(bf16[1,512,3584]{2,1,0:T(8,128)(2,1)S(1)} %copy-done.2, bf16[64,3584]{1,0:T(8,128)(2,1)S(1)} %get-tuple-element.31, bf16[64,3584]{1,0:T(8,128)(2,1)S(1)} %get-tuple-element.30), kind=kOutput, calls=%fused_computation.9 | convolution fusion | flops 471662592 | bytes 4718592 | tf_op jit(solution)/shard_map/td,hd->th/dot_general | solution.py:104
  87.8 0.7 maximum_bitcast_fusion
  88.5 10.7 %all-to-all-done = bf16[16,24,896]{2,1,0:T(8,128)(2,1)S(1)} async-done(((bf16[16,24,896]{2,1,0:T(8,128)(2,1)}), bf16[16,24,896]{2,1,0:T(8,128)(2,1)S(1)}, u32[]{:S(2)}, u32[]{:S(2)}) %all-to-all-start) | async-done | bytes 688160 | tf_op jit(solution)/shard_map/all_to_all | solution.py:45
  99.2 1.3 %reshape_reshape.3 = bf16[1,1,1,96,3584]{4,3,2,1,0:T(8,128)(2,1)} reshape(bf16[16,24,896]{2,1,0:T(8,128)(2,1)S(1)} %all-to-all-done) | data formatting | bytes 1376256 | tf_op jit(solution)/shard_map/reshape;reshape | solution.py:111
  (17 shorter events, 0.3 us)
Async XLA Ops:
  0.6 28.1 %copy-start = (s32[2,1,64,1]{2,3,1,0:T(1,128)S(1)}, s32[2,1,64,1]{2,3,1,0:T(1,128)}, u32[]{:S(2)}) copy-start(s32[2,1,64,1]{2,3,1,0:T(1,128)} %param.6) | copy-start | bytes 1540
  0.6 37.8 %copy-start.1 = (f32[1,64]{1,0:T(1,128)S(1)}, f32[1,64]{1,0:T(1,128)}, u32[]{:S(2)}) copy-start(f32[1,64]{1,0:T(1,128)} %param.7) | copy-start | bytes 772
  2.9 53.8 %all-to-all-start.1 = ((bf16[16,24,896]{2,1,0:T(8,128)(2,1)}), bf16[16,24,896]{2,1,0:T(8,128)(2,1)S(1)}, u32[]{:S(2)}, u32[]{:S(2)}) async-start(bf16[16,24,896]{2,1,0:T(8,128)(2,1)} %reshape_squeeze.3), calls=%async_computation.1 | async-start | bytes 1376256 | tf_op jit(solution)/shard_map/all_to_all | solution.py:45
  23.0 15.4 %collective-permute-start = (bf16[64,3584]{1,0:T(8,128)(2,1)S(1)}, bf16[64,3584]{1,0:T(8,128)(2,1)S(1)}, u32[]{:S(2)}, u32[]{:S(2)}) collective-permute-start(bf16[64,3584]{1,0:T(8,128)(2,1)S(1)} %get-tuple-element.32), channel_id=1, source_target_pairs={{64,0},{128,64},{192,128},{256,192},{320,256},{384,320},{448,384},... | collective-permute-start | bytes 1376264 | tf_op jit(solution)/shard_map/ppermute | solution.py:13
  38.6 3.9 %collective-permute-start.1 = (bf16[72,3584]{1,0:T(8,128)(2,1)S(1)}, bf16[72,3584]{1,0:T(8,128)(2,1)S(1)}, u32[]{:S(2)}, u32[]{:S(2)}) collective-permute-start(bf16[72,3584]{1,0:T(8,128)(2,1)S(1)} %fusion.23), channel_id=1, source_target_pairs={{0,2},{2,0},{4,6},{6,4},{8,10},{10,8},{12,14},{14,12},{16,18},{18,... | collective-permute-start | bytes 1548296 | tf_op jit(solution)/shard_map/ppermute | solution.py:18
  40.6 24.1 %collective-permute-start.2 = (bf16[64,3584]{1,0:T(8,128)(2,1)S(1)}, bf16[64,3584]{1,0:T(8,128)(2,1)S(1)}, u32[]{:S(2)}, u32[]{:S(2)}) collective-permute-start(bf16[64,3584]{1,0:T(8,128)(2,1)S(1)} %get-tuple-element.12), channel_id=1, source_target_pairs={{0,64},{64,128},{128,192},{192,256},{256,320},{320,384},{384,448},... | collective-permute-start | bytes 1376264 | tf_op jit(solution)/shard_map/ppermute | solution.py:13
  44.2 22.7 %collective-permute-start.4 = (bf16[64,3584]{1,0:T(8,128)(2,1)S(1)}, bf16[64,3584]{1,0:T(8,128)(2,1)}, u32[]{:S(2)}, u32[]{:S(2)}) collective-permute-start(bf16[64,3584]{1,0:T(8,128)(2,1)S(1)} %collective-permute-done), channel_id=1, source_target_pairs={{0,1},{1,0},{2,3},{3,2},{4,5},{5,4},{6,7},{7,6},{8,9},{9,8},{10,11... | collective-permute-start | bytes 1376264 | tf_op jit(solution)/shard_map/ppermute | solution.py:18
  56.8 42.5 %all-to-all-start = ((bf16[16,24,896]{2,1,0:T(8,128)(2,1)}), bf16[16,24,896]{2,1,0:T(8,128)(2,1)S(1)}, u32[]{:S(2)}, u32[]{:S(2)}) async-start(bf16[16,24,896]{2,1,0:T(8,128)(2,1)} %bitcast.7), calls=%async_computation | async-start | bytes 1376256 | tf_op jit(solution)/shard_map/all_to_all | solution.py:45
  64.9 10.1 %collective-permute-start.3 = (bf16[48,3584]{1,0:T(8,128)(2,1)S(1)}, bf16[48,3584]{1,0:T(8,128)(2,1)S(1)}, u32[]{:S(2)}, u32[]{:S(2)}) collective-permute-start(bf16[48,3584]{1,0:T(8,128)(2,1)S(1)} %convolution_convert_fusion), channel_id=1, source_target_pairs={{0,2},{2,0},{4,6},{6,4},{8,10},{10,8},{12,14},{14,12},{16,18},{18,... | collective-permute-start | bytes 1032200 | tf_op jit(solution)/shard_map/ppermute | solution.py:18
  71.3 15.2 %copy-start.2 = (bf16[1,512,3584]{2,1,0:T(8,128)(2,1)S(1)}, bf16[1,512,3584]{2,1,0:T(8,128)(2,1)}, u32[]{:S(2)}) copy-start(bf16[1,512,3584]{2,1,0:T(8,128)(2,1)} %param.9) | copy-start | bytes 11010052
  71.3 15.1 %collective-permute-start.5 = (bf16[64,3584]{1,0:T(8,128)(2,1)S(1)}, bf16[64,3584]{1,0:T(8,128)(2,1)S(1)}, u32[]{:S(2)}, u32[]{:S(2)}) collective-permute-start(bf16[64,3584]{1,0:T(8,128)(2,1)S(1)} %collective-permute-done.2), channel_id=1, source_target_pairs={{0,1},{1,0},{2,3},{3,2},{4,5},{5,4},{6,7},{7,6},{8,9},{9,8},{10,11... | collective-permute-start | bytes 1376264 | tf_op jit(solution)/shard_map/ppermute | solution.py:18

commit v4 on v3

--- a/solution.py
+++ b/solution.py
@@ -1,10 +1,13 @@
 import jax
 import jax.numpy as jnp
 from jax import lax
+from jax.experimental import pallas as pl
+from jax.experimental.pallas import tpu as pltpu
 from jax.sharding import PartitionSpec as P
 
 CORES = 2
 PARTS = 4
+CHUNK = 32
 
 
 def shifted(array, axis, by):
@@ -28,6 +31,46 @@
 
 def select(rows, width, dtype=jnp.bfloat16):
     return (rows[:, None] == jnp.arange(width, dtype=jnp.int32)[None, :]).astype(dtype)
+
+
+def from_lines(lines):
+    total, part = lines.shape
+    count, width = total // PARTS, part * PARTS
+    chunks, block = count // CHUNK, CHUNK * PARTS
+
+    def kernel(lines_ref, rows_ref, result, out_sem):
+        line = lax.broadcasted_iota(jnp.int32, (block, block), 1)
+        column = lax.broadcasted_iota(jnp.int32, (block, block), 0)
+        table = (column == (line % PARTS) * CHUNK + line // PARTS).astype(jnp.bfloat16)
+        leaving = []
+        for q in range(chunks):
+            moved = jnp.dot(
+                table, lines_ref[q * block : (q + 1) * block], preferred_element_type=jnp.float32
+            ).astype(jnp.bfloat16)
+            for g in range(PARTS):
+                result[q, :, g * part : (g + 1) * part] = moved[g * CHUNK : (g + 1) * CHUNK]
+            copy = pltpu.make_async_copy(
+                result.at[q], rows_ref.at[pl.ds(q * CHUNK, CHUNK)], out_sem.at[q]
+            )
+            copy.start()
+            leaving.append(copy)
+        for copy in leaving:
+            copy.wait()
+
+    return pl.pallas_call(
+        kernel,
+        out_shape=jax.ShapeDtypeStruct((count, width), lines.dtype),
+        in_specs=[pl.BlockSpec(memory_space=pltpu.VMEM)],
+        out_specs=pl.BlockSpec(memory_space=pl.ANY),
+        scratch_shapes=[
+            pltpu.VMEM((chunks, CHUNK, width), lines.dtype),
+            pltpu.SemaphoreType.DMA((chunks,)),
+        ],
+        compiler_params=pltpu.CompilerParams(vmem_limit_bytes=16 << 20),
+        cost_estimate=pl.CostEstimate(
+            flops=2 * count * width * block, bytes_accessed=4 * count * width, transcendentals=0
+        ),
+    )(lines)
 
 
 def on_device(grad_in, expert_ids, gate_weights, back_rows, shared_down):
@@ -77,7 +120,7 @@
     table = (line[:, None] == target[None, :]).astype(jnp.bfloat16)
     packed = jnp.dot(table, spread, preferred_element_type=jnp.float32).astype(jnp.bfloat16)
     packed = packed.reshape(chips, chip_rows * PARTS, part)
-    sent = exchanged(packed).reshape(buffer_rows, width)
+    sent = from_lines(exchanged(packed).reshape(buffer_rows * PARTS, part))
     from_prev, came = lax.optimization_barrier((from_prev, came))
 
     lines = jnp.arange(chips * cap, dtype=jnp.int32)

time: 101 us -> 101 us (level)
  local copies, waits for them, and re-layouts: 5.31 us -> 4.06 us
  Pallas kernels: 0 us -> 1.08 us
    another operation x1 -> x0, local copies, waits for them, and re-layouts: 1.26 us -> none  [on_device(): sent.reshape(1, 1, 1, buffer_rows, width)]
    pallas_call x0 -> x1, Pallas kernels: none -> 1.08 us  [from_lines(): pl.pallas_call(kernel, out_shape=jax.ShapeDtypeStruct((count, width), lin...]
where the time goes in v4:
time: 101 us; the launch traced here: 100 us
  starting transfers between devices  44.8 us (44%)
  waiting for transfers between devices  39.1 us (39%)
  matrix products  7.77 us (8%)
  local copies, waits for them, and re-layouts  4.06 us (4%)
  other arithmetic  2.57 us (3%)
  Pallas kernels  1.08 us (1%)
    all_to_all x2, starting transfers between devices, exchanged(): lax.all_to_all(pieces, 'expert', split_axis=0, concat_axis=0, tiled=True,...  26.3 us
    all_to_all x2, waiting for transfers between devices, exchanged(): lax.all_to_all(pieces, 'expert', split_axis=0, concat_axis=0, tiled=True,...  19.9 us
    ppermute x4, starting transfers between devices, swapped(): return lax.ppermute(array, axis, [(i, i ^ 1) for i in range(peers)])  10.9 us
    ppermute x4, waiting for transfers between devices, swapped(): return lax.ppermute(array, axis, [(i, i ^ 1) for i in range(peers)])  9.97 us
    ppermute x2, waiting for transfers between devices, shifted(): return lax.ppermute(array, axis, pairs)  9.23 us
    ppermute x2, starting transfers between devices, shifted(): return lax.ppermute(array, axis, pairs)  7.64 us
    dot_general x2, matrix products, hidden(): jnp.einsum('td,hd->th', tokens, down_part, preferred_element_type=jnp.flo...  4.63 us
    another operation x1, local copies, waits for them, and re-layouts, on_device(): pieces = back_rows[0, 0, 0].reshape(chips, chip_rows * PARTS, part)  2.28 us
  transfers between devices with their start and end apart: 8, of which 4 were waited for; matrix products, arithmetic and copies ran while one was open for 12% of the time, Pallas kernels for 0%

profile of v4, /device:TPU:56, one launch (start us, length us, event | category | flops | bytes accessed | tf_op | source)
XLA Modules:
  0.0 100.3 jit_solution(1789608554254053931)
XLA Ops:
  0.6 0.0 copy-start
  0.6 0.0 copy-start.1
  0.7 2.3 %reshape_squeeze.3 = bf16[16,24,896]{2,1,0:T(8,128)(2,1)} reshape(bf16[1,1,1,96,3584]{4,3,2,1,0:T(8,128)(2,1)} %param.8) | data formatting | bytes 1376256 | tf_op jit(solution)/shard_map/reshape;squeeze | solution.py:92
  2.9 18.9 %all-to-all-start.1 = ((bf16[16,24,896]{2,1,0:T(8,128)(2,1)}), bf16[16,24,896]{2,1,0:T(8,128)(2,1)S(1)}, u32[]{:S(2)}, u32[]{:S(2)}) async-start(bf16[16,24,896]{2,1,0:T(8,128)(2,1)} %reshape_squeeze.3), calls=%async_computation.1 | async-start | bytes 1376256 | tf_op jit(solution)/shard_map/all_to_all | solution.py:88
  21.8 1.2 %slice_bitcast_fusion = (bf16[64,3584]{1,0:T(8,128)(2,1)S(1)}, bf16[64,3584]{1,0:T(8,128)(2,1)S(1)}) fusion(bf16[2,1,64,3584]{3,2,1,0:T(8,128)(2,1)} %param.5), kind=kLoop, calls=%fused_computation.24 | loop fusion | bytes 1835008 | tf_op jit(solution)/shard_map/squeeze | solution.py:94
  23.0 5.7 %collective-permute-start = (bf16[64,3584]{1,0:T(8,128)(2,1)S(1)}, bf16[64,3584]{1,0:T(8,128)(2,1)S(1)}, u32[]{:S(2)}, u32[]{:S(2)}) collective-permute-start(bf16[64,3584]{1,0:T(8,128)(2,1)S(1)} %get-tuple-element.32), channel_id=1, source_target_pairs={{64,0},{128,64},{192,128},{256,192},{320,256},{384,320},{448,384},... | collective-permute-start | bytes 1376264 | tf_op jit(solution)/shard_map/ppermute | solution.py:16
  28.7 0.0 copy-done
  28.8 0.2 convert_reduce_fusion
  29.0 0.2 convert_reduce_fusion.1
  29.2 9.2 %collective-permute-done = bf16[64,3584]{1,0:T(8,128)(2,1)S(1)} collective-permute-done((bf16[64,3584]{1,0:T(8,128)(2,1)S(1)}, bf16[64,3584]{1,0:T(8,128)(2,1)S(1)}, u32[]{:S(2)}, u32[]{:S(2)}) %collective-permute-start) | collective-permute-done | bytes 458784 | tf_op jit(solution)/shard_map/ppermute | solution.py:16
  38.4 0.0 copy-done.1
  38.4 0.1 multiply_convert_fusion
  38.6 1.9 %collective-permute-start.1 = (bf16[72,3584]{1,0:T(8,128)(2,1)S(1)}, bf16[72,3584]{1,0:T(8,128)(2,1)S(1)}, u32[]{:S(2)}, u32[]{:S(2)}) collective-permute-start(bf16[72,3584]{1,0:T(8,128)(2,1)S(1)} %fusion.23), channel_id=1, source_target_pairs={{0,2},{2,0},{4,6},{6,4},{8,10},{10,8},{12,14},{14,12},{16,18},{18,... | collective-permute-start | bytes 1548296 | tf_op jit(solution)/shard_map/ppermute | solution.py:21
  40.6 1.9 %collective-permute-start.2 = (bf16[64,3584]{1,0:T(8,128)(2,1)S(1)}, bf16[64,3584]{1,0:T(8,128)(2,1)S(1)}, u32[]{:S(2)}, u32[]{:S(2)}) collective-permute-start(bf16[64,3584]{1,0:T(8,128)(2,1)S(1)} %get-tuple-element.12), channel_id=1, source_target_pairs={{0,64},{64,128},{128,192},{192,256},{256,320},{320,384},{384,448},... | collective-permute-start | bytes 1376264 | tf_op jit(solution)/shard_map/ppermute | solution.py:16
  42.5 0.0 collective-permute-done.1
  42.5 0.1 broadcast_add_fusion.2
  42.8 1.4 %convolution_convert_fusion.1 = bf16[384,896]{1,0:T(8,128)(2,1)} fusion(bf16[512,896]{1,0:T(8,128)(2,1)S(1)} %slice_dynamic-update-slice_fusion, s32[512]{0:T(512)S(1)} %pad_add_fusion), kind=kOutput, calls=%fused_computation.6 | convolution fusion | flops 352862208 | bytes 1607680 | tf_op jit(solution)/shard_map/dot_general | solution.py:121
  44.2 3.4 %collective-permute-start.4 = (bf16[64,3584]{1,0:T(8,128)(2,1)S(1)}, bf16[64,3584]{1,0:T(8,128)(2,1)}, u32[]{:S(2)}, u32[]{:S(2)}) collective-permute-start(bf16[64,3584]{1,0:T(8,128)(2,1)S(1)} %collective-permute-done), channel_id=1, source_target_pairs={{0,1},{1,0},{2,3},{3,2},{4,5},{5,4},{6,7},{7,6},{8,9},{9,8},{10,11... | collective-permute-start | bytes 1376264 | tf_op jit(solution)/shard_map/ppermute | solution.py:21
  47.6 9.1 %all-to-all-done.1 = bf16[16,24,896]{2,1,0:T(8,128)(2,1)S(1)} async-done(((bf16[16,24,896]{2,1,0:T(8,128)(2,1)}), bf16[16,24,896]{2,1,0:T(8,128)(2,1)S(1)}, u32[]{:S(2)}, u32[]{:S(2)}) %all-to-all-start.1) | async-done | bytes 688160 | tf_op jit(solution)/shard_map/all_to_all | solution.py:88
  56.8 7.4 %all-to-all-start = ((bf16[16,24,896]{2,1,0:T(8,128)(2,1)}), bf16[16,24,896]{2,1,0:T(8,128)(2,1)S(1)}, u32[]{:S(2)}, u32[]{:S(2)}) async-start(bf16[16,24,896]{2,1,0:T(8,128)(2,1)} %bitcast.7), calls=%async_computation | async-start | bytes 1376256 | tf_op jit(solution)/shard_map/all_to_all | solution.py:88
  64.2 0.4 reshape.241
  64.6 0.0 collective-permute-done.2
  64.6 0.3 convolution_convert_fusion
  64.9 1.9 %collective-permute-start.3 = (bf16[48,3584]{1,0:T(8,128)(2,1)S(1)}, bf16[48,3584]{1,0:T(8,128)(2,1)S(1)}, u32[]{:S(2)}, u32[]{:S(2)}) collective-permute-start(bf16[48,3584]{1,0:T(8,128)(2,1)S(1)} %convolution_convert_fusion), channel_id=1, source_target_pairs={{0,2},{2,0},{4,6},{6,4},{8,10},{10,8},{12,14},{14,12},{16,18},{18,... | collective-permute-start | bytes 1032200 | tf_op jit(solution)/shard_map/ppermute | solution.py:21
  66.9 0.0 collective-permute-done.4
  66.9 1.1 %broadcast_select_fusion.3 = (bf16[64,3584]{1,0:T(8,128)(2,1)S(1)}, bf16[64,3584]{1,0:T(8,128)(2,1)S(1)}) fusion(bf16[64,3584]{1,0:T(8,128)(2,1)S(1)} %collective-permute-done, bf16[64,3584]{1,0:T(8,128)(2,1)} %collective-permute-done.4, pred[]{:T(512)S(6)} %eq.142), kind=kLoop, calls=%fused_computation.29 | loop fusion | flops 458752 | bytes 1835009 | tf_op jit(solution)/shard_map/jit(_where)/select_n | solution.py:144
  68.0 3.3 %fusion.13 = bf16[1,128,512]{2,1,0:T(8,128)(2,1)S(1)} fusion(bf16[1,512,3584]{2,1,0:T(8,128)(2,1)} %param.9, bf16[64,3584]{1,0:T(8,128)(2,1)S(1)} %get-tuple-element.29, bf16[64,3584]{1,0:T(8,128)(2,1)S(1)} %get-tuple-element.28), kind=kOutput, calls=%fused_computation.10 | convolution fusion | flops 471662592 | bytes 4718592 | tf_op jit(solution)/shard_map/td,hd->th/dot_general | solution.py:147
  71.3 0.0 copy-start.2
  71.3 3.7 %collective-permute-start.5 = (bf16[64,3584]{1,0:T(8,128)(2,1)S(1)}, bf16[64,3584]{1,0:T(8,128)(2,1)S(1)}, u32[]{:S(2)}, u32[]{:S(2)}) collective-permute-start(bf16[64,3584]{1,0:T(8,128)(2,1)S(1)} %collective-permute-done.2), channel_id=1, source_target_pairs={{0,1},{1,0},{2,3},{3,2},{4,5},{5,4},{6,7},{7,6},{8,9},{9,8},{10,11... | collective-permute-start | bytes 1376264 | tf_op jit(solution)/shard_map/ppermute | solution.py:21
  75.0 0.0 collective-permute-done.3
  75.0 0.3 fusion.28
  75.3 1.1 %fusion.24 = bf16[1,64,3584]{2,1,0:T(8,128)(2,1)} fusion(bf16[64,3584]{1,0:T(8,128)(2,1)S(1)} %collective-permute-done.2, f32[64,3584]{1,0:T(8,128)S(1)} %fusion.28, bf16[96,3584]{1,0:T(8,128)(2,1)S(1)} %reshape.241, s32[64]{0:T(128)S(1)} %get-tuple-element.23), kind=kOutput, calls=%fused_computation.23 | convolution fusion | flops 44963840 | bytes 2523392 | tf_op jit(solution)/shard_map/dot_general | solution.py:134
  76.4 10.0 %collective-permute-done.5 = bf16[64,3584]{1,0:T(8,128)(2,1)S(1)} collective-permute-done((bf16[64,3584]{1,0:T(8,128)(2,1)S(1)}, bf16[64,3584]{1,0:T(8,128)(2,1)S(1)}, u32[]{:S(2)}, u32[]{:S(2)}) %collective-permute-start.5) | collective-permute-done | bytes 458784 | tf_op jit(solution)/shard_map/ppermute | solution.py:21
  86.4 0.1 broadcast_select_fusion.1
  86.5 0.0 copy-done.2
  86.5 1.3 %fusion.10 = bf16[1,128,512]{2,1,0:T(8,128)(2,1)S(1)} fusion(bf16[1,512,3584]{2,1,0:T(8,128)(2,1)S(1)} %copy-done.2, bf16[64,3584]{1,0:T(8,128)(2,1)S(1)} %get-tuple-element.31, bf16[64,3584]{1,0:T(8,128)(2,1)S(1)} %get-tuple-element.30), kind=kOutput, calls=%fused_computation.9 | convolution fusion | flops 471662592 | bytes 4718592 | tf_op jit(solution)/shard_map/td,hd->th/dot_general | solution.py:147
  87.8 0.7 maximum_bitcast_fusion
  88.5 10.7 %all-to-all-done = bf16[16,24,896]{2,1,0:T(8,128)(2,1)S(1)} async-done(((bf16[16,24,896]{2,1,0:T(8,128)(2,1)}), bf16[16,24,896]{2,1,0:T(8,128)(2,1)S(1)}, u32[]{:S(2)}, u32[]{:S(2)}) %all-to-all-start) | async-done | bytes 688160 | tf_op jit(solution)/shard_map/all_to_all | solution.py:88
  99.2 1.1 %shard_map.76 = bf16[96,3584]{1,0:T(8,128)(2,1)} custom-call(bf16[384,896]{1,0:T(8,128)(2,1)S(1)} %bitcast.75), custom_call_target="tpu_custom_call" | custom-call | flops 88080384 | bytes 1376256 | tf_op jit(solution)/shard_map/pallas_call | solution.py:60
  (17 shorter events, 0.3 us)
Async XLA Ops:
  0.6 28.1 %copy-start = (s32[2,1,64,1]{2,3,1,0:T(1,128)S(1)}, s32[2,1,64,1]{2,3,1,0:T(1,128)}, u32[]{:S(2)}) copy-start(s32[2,1,64,1]{2,3,1,0:T(1,128)} %param.6) | copy-start | bytes 1540
  0.6 37.8 %copy-start.1 = (f32[1,64]{1,0:T(1,128)S(1)}, f32[1,64]{1,0:T(1,128)}, u32[]{:S(2)}) copy-start(f32[1,64]{1,0:T(1,128)} %param.7) | copy-start | bytes 772
  2.9 53.8 %all-to-all-start.1 = ((bf16[16,24,896]{2,1,0:T(8,128)(2,1)}), bf16[16,24,896]{2,1,0:T(8,128)(2,1)S(1)}, u32[]{:S(2)}, u32[]{:S(2)}) async-start(bf16[16,24,896]{2,1,0:T(8,128)(2,1)} %reshape_squeeze.3), calls=%async_computation.1 | async-start | bytes 1376256 | tf_op jit(solution)/shard_map/all_to_all | solution.py:88
  23.0 15.4 %collective-permute-start = (bf16[64,3584]{1,0:T(8,128)(2,1)S(1)}, bf16[64,3584]{1,0:T(8,128)(2,1)S(1)}, u32[]{:S(2)}, u32[]{:S(2)}) collective-permute-start(bf16[64,3584]{1,0:T(8,128)(2,1)S(1)} %get-tuple-element.32), channel_id=1, source_target_pairs={{64,0},{128,64},{192,128},{256,192},{320,256},{384,320},{448,384},... | collective-permute-start | bytes 1376264 | tf_op jit(solution)/shard_map/ppermute | solution.py:16
  38.6 3.9 %collective-permute-start.1 = (bf16[72,3584]{1,0:T(8,128)(2,1)S(1)}, bf16[72,3584]{1,0:T(8,128)(2,1)S(1)}, u32[]{:S(2)}, u32[]{:S(2)}) collective-permute-start(bf16[72,3584]{1,0:T(8,128)(2,1)S(1)} %fusion.23), channel_id=1, source_target_pairs={{0,2},{2,0},{4,6},{6,4},{8,10},{10,8},{12,14},{14,12},{16,18},{18,... | collective-permute-start | bytes 1548296 | tf_op jit(solution)/shard_map/ppermute | solution.py:21
  40.6 24.1 %collective-permute-start.2 = (bf16[64,3584]{1,0:T(8,128)(2,1)S(1)}, bf16[64,3584]{1,0:T(8,128)(2,1)S(1)}, u32[]{:S(2)}, u32[]{:S(2)}) collective-permute-start(bf16[64,3584]{1,0:T(8,128)(2,1)S(1)} %get-tuple-element.12), channel_id=1, source_target_pairs={{0,64},{64,128},{128,192},{192,256},{256,320},{320,384},{384,448},... | collective-permute-start | bytes 1376264 | tf_op jit(solution)/shard_map/ppermute | solution.py:16
  44.2 22.7 %collective-permute-start.4 = (bf16[64,3584]{1,0:T(8,128)(2,1)S(1)}, bf16[64,3584]{1,0:T(8,128)(2,1)}, u32[]{:S(2)}, u32[]{:S(2)}) collective-permute-start(bf16[64,3584]{1,0:T(8,128)(2,1)S(1)} %collective-permute-done), channel_id=1, source_target_pairs={{0,1},{1,0},{2,3},{3,2},{4,5},{5,4},{6,7},{7,6},{8,9},{9,8},{10,11... | collective-permute-start | bytes 1376264 | tf_op jit(solution)/shard_map/ppermute | solution.py:21
  56.8 42.5 %all-to-all-start = ((bf16[16,24,896]{2,1,0:T(8,128)(2,1)}), bf16[16,24,896]{2,1,0:T(8,128)(2,1)S(1)}, u32[]{:S(2)}, u32[]{:S(2)}) async-start(bf16[16,24,896]{2,1,0:T(8,128)(2,1)} %bitcast.7), calls=%async_computation | async-start | bytes 1376256 | tf_op jit(solution)/shard_map/all_to_all | solution.py:88
  64.9 10.1 %collective-permute-start.3 = (bf16[48,3584]{1,0:T(8,128)(2,1)S(1)}, bf16[48,3584]{1,0:T(8,128)(2,1)S(1)}, u32[]{:S(2)}, u32[]{:S(2)}) collective-permute-start(bf16[48,3584]{1,0:T(8,128)(2,1)S(1)} %convolution_convert_fusion), channel_id=1, source_target_pairs={{0,2},{2,0},{4,6},{6,4},{8,10},{10,8},{12,14},{14,12},{16,18},{18,... | collective-permute-start | bytes 1032200 | tf_op jit(solution)/shard_map/ppermute | solution.py:21
  71.3 15.2 %copy-start.2 = (bf16[1,512,3584]{2,1,0:T(8,128)(2,1)S(1)}, bf16[1,512,3584]{2,1,0:T(8,128)(2,1)}, u32[]{:S(2)}) copy-start(bf16[1,512,3584]{2,1,0:T(8,128)(2,1)} %param.9) | copy-start | bytes 11010052
  71.3 15.1 %collective-permute-start.5 = (bf16[64,3584]{1,0:T(8,128)(2,1)S(1)}, bf16[64,3584]{1,0:T(8,128)(2,1)S(1)}, u32[]{:S(2)}, u32[]{:S(2)}) collective-permute-start(bf16[64,3584]{1,0:T(8,128)(2,1)S(1)} %collective-permute-done.2), channel_id=1, source_target_pairs={{0,1},{1,0},{2,3},{3,2},{4,5},{5,4},{6,7},{7,6},{8,9},{9,8},{10,11... | collective-permute-start | bytes 1376264 | tf_op jit(solution)/shard_map/ppermute | solution.py:21

commit v5 on v4

--- a/solution.py
+++ b/solution.py
@@ -89,7 +89,13 @@
             pieces, "expert", split_axis=0, concat_axis=0, tiled=True, axis_index_groups=across
         )
 
-    pieces = back_rows[0, 0, 0].reshape(chips, chip_rows * PARTS, part)
+    total = buffer_rows * PARTS
+    order = jnp.arange(total, dtype=jnp.int32)
+    order = (order % PARTS) * buffer_rows + order // PARTS
+    back = back_rows[0, 0, 0]
+    back = jnp.concatenate([back[:, g * part : (g + 1) * part] for g in range(PARTS)], axis=0)
+    pieces = jnp.dot(select(order, total), back, preferred_element_type=jnp.float32)
+    pieces = pieces.astype(jnp.bfloat16).reshape(chips, chip_rows * PARTS, part)
     pieces, grads = lax.optimization_barrier((pieces, grad_in))
     own_a = grads[0, 0]
     came = exchanged(pieces)

time: 101 us -> 102 us (level)
  local copies, waits for them, and re-layouts: 4.06 us -> 1.86 us
  matrix products: 7.77 us -> 9.21 us
  waiting for transfers between devices: 39.1 us -> 40.5 us
    another operation x1 -> x0, local copies, waits for them, and re-layouts: 2.28 us -> none  [on_device(): pieces = back_rows[0, 0, 0].reshape(chips, chip_rows * PARTS, part)]
    dot_general x0 -> x1, matrix products: none -> 1.44 us  [on_device(): jnp.dot(select(order, total), back, preferred_element_type=jnp.float32)]
    all_to_all x2, waiting for transfers between devices: 19.9 us -> 21.3 us  [exchanged(): lax.all_to_all(pieces, 'expert', split_axis=0, concat_axis=0, tiled=True,...]
    slice x0 -> x1, local copies, waits for them, and re-layouts: none -> 1.23 us  [on_device(): back[:, g * part:(g + 1) * part]]
    squeeze x1, local copies, waits for them, and re-layouts: 1.22 us -> 0.06 us  [on_device(): own_a = grads[0, 0]]
  transfers between devices with their start and end apart: 8 -> 8, of which waited for: 4 -> 4; matrix products, arithmetic and copies ran while one was open for 12% -> 11% of each run, Pallas kernels for 0% -> 0%
where the time goes in v5:
time: 102 us; the launch traced here: 101 us
  starting transfers between devices  44.7 us (44%)
  waiting for transfers between devices  40.5 us (40%)
  matrix products  9.21 us (9%)
  other arithmetic  2.58 us (3%)
  local copies, waits for them, and re-layouts  1.86 us (2%)
  Pallas kernels  1.08 us (1%)
    all_to_all x2, starting transfers between devices, exchanged(): lax.all_to_all(pieces, 'expert', split_axis=0, concat_axis=0, tiled=True,...  26.4 us
    all_to_all x2, waiting for transfers between devices, exchanged(): lax.all_to_all(pieces, 'expert', split_axis=0, concat_axis=0, tiled=True,...  21.3 us
    ppermute x4, starting transfers between devices, swapped(): return lax.ppermute(array, axis, [(i, i ^ 1) for i in range(peers)])  10.6 us
    ppermute x4, waiting for transfers between devices, swapped(): return lax.ppermute(array, axis, [(i, i ^ 1) for i in range(peers)])  9.97 us
    ppermute x2, waiting for transfers between devices, shifted(): return lax.ppermute(array, axis, pairs)  9.23 us
    ppermute x2, starting transfers between devices, shifted(): return lax.ppermute(array, axis, pairs)  7.64 us
    dot_general x2, matrix products, hidden(): jnp.einsum('td,hd->th', tokens, down_part, preferred_element_type=jnp.flo...  4.62 us
  transfers between devices with their start and end apart: 8, of which 4 were waited for; matrix products, arithmetic and copies ran while one was open for 11% of the time, Pallas kernels for 0%

profile of v5, /device:TPU:56, one launch (start us, length us, event | category | flops | bytes accessed | tf_op | source)
XLA Modules:
  0.0 100.9 jit_solution(6626784192104448197)
XLA Ops:
  0.6 1.2 %fusion.57 = (bf16[96,896]{1,0:T(8,128)(2,1)S(1)}, bf16[96,896]{1,0:T(8,128)(2,1)S(1)}, bf16[96,896]{1,0:T(8,128)(2,1)S(1)}, bf16[96,896]{1,0:T(8,128)(2,1)S(1)}) fusion(bf16[96,3584]{1,0:T(8,128)(2,1)} %bitcast.76), kind=kLoop, calls=%fused_computation.117 | loop fusion | bytes 1376256 | tf_op jit(solution)/shard_map/slice | solution.py:96
  1.9 0.0 copy-start
  1.9 1.4 %convolution_convert_fusion.1 = bf16[384,896]{1,0:T(8,128)(2,1)} fusion(bf16[96,896]{1,0:T(8,128)(2,1)S(1)} %get-tuple-element.35, bf16[96,896]{1,0:T(8,128)(2,1)S(1)} %get-tuple-element.36, bf16[96,896]{1,0:T(8,128)(2,1)S(1)} %get-tuple-element.37, bf16[96,896]{1,0:T(8,128)(2,1)S(1)} %get-tuple-element.34, s32[384]{0:T(512)S(1)} %fusion.44), kind=kOutput, calls=%fused_computation.6 | convolution fusion | flops 267485184 | bytes 1377792 | tf_op jit(solution)/shard_map/dot_general | solution.py:97
  3.3 0.0 copy-start.1
  3.3 0.0 copy-start.2
  3.3 19.0 %all-to-all-start.1 = ((bf16[16,24,896]{2,1,0:T(8,128)(2,1)}), bf16[16,24,896]{2,1,0:T(8,128)(2,1)S(1)}, u32[]{:S(2)}, u32[]{:S(2)}) async-start(bf16[16,24,896]{2,1,0:T(8,128)(2,1)} %bitcast.3), calls=%async_computation.1 | async-start | bytes 1376256 | tf_op jit(solution)/shard_map/all_to_all | solution.py:88
  22.3 0.0 copy-done
  22.3 0.1 slice_bitcast_fusion
  22.4 5.7 %collective-permute-start = (bf16[64,3584]{1,0:T(8,128)(2,1)S(1)}, bf16[64,3584]{1,0:T(8,128)(2,1)S(1)}, u32[]{:S(2)}, u32[]{:S(2)}) collective-permute-start(bf16[64,3584]{1,0:T(8,128)(2,1)S(1)} %get-tuple-element.32), channel_id=1, source_target_pairs={{64,0},{128,64},{192,128},{256,192},{320,256},{384,320},{448,384},... | collective-permute-start | bytes 1376264 | tf_op jit(solution)/shard_map/ppermute | solution.py:16
  28.1 0.0 copy-done.1
  28.2 0.2 convert_reduce_fusion
  28.3 0.2 convert_reduce_fusion.1
  28.6 9.2 %collective-permute-done = bf16[64,3584]{1,0:T(8,128)(2,1)S(1)} collective-permute-done((bf16[64,3584]{1,0:T(8,128)(2,1)S(1)}, bf16[64,3584]{1,0:T(8,128)(2,1)S(1)}, u32[]{:S(2)}, u32[]{:S(2)}) %collective-permute-start) | collective-permute-done | bytes 458784 | tf_op jit(solution)/shard_map/ppermute | solution.py:16
  37.8 0.0 copy-done.2
  37.8 0.1 multiply_convert_fusion
  38.0 1.9 %collective-permute-start.1 = (bf16[72,3584]{1,0:T(8,128)(2,1)S(1)}, bf16[72,3584]{1,0:T(8,128)(2,1)S(1)}, u32[]{:S(2)}, u32[]{:S(2)}) collective-permute-start(bf16[72,3584]{1,0:T(8,128)(2,1)S(1)} %fusion.30), channel_id=1, source_target_pairs={{0,2},{2,0},{4,6},{6,4},{8,10},{10,8},{12,14},{14,12},{16,18},{18,... | collective-permute-start | bytes 1548296 | tf_op jit(solution)/shard_map/ppermute | solution.py:21
  40.0 1.9 %collective-permute-start.2 = (bf16[64,3584]{1,0:T(8,128)(2,1)S(1)}, bf16[64,3584]{1,0:T(8,128)(2,1)S(1)}, u32[]{:S(2)}, u32[]{:S(2)}) collective-permute-start(bf16[64,3584]{1,0:T(8,128)(2,1)S(1)} %get-tuple-element.12), channel_id=1, source_target_pairs={{0,64},{64,128},{128,192},{192,256},{256,320},{320,384},{384,448},... | collective-permute-start | bytes 1376264 | tf_op jit(solution)/shard_map/ppermute | solution.py:16
  41.9 0.0 collective-permute-done.1
  41.9 0.1 broadcast_add_fusion.2
  42.2 1.4 %convolution_convert_fusion.2 = bf16[384,896]{1,0:T(8,128)(2,1)} fusion(bf16[512,896]{1,0:T(8,128)(2,1)S(1)} %slice_dynamic-update-slice_fusion, s32[512]{0:T(512)S(1)} %pad_add_fusion), kind=kOutput, calls=%fused_computation.7 | convolution fusion | flops 352862208 | bytes 1607680 | tf_op jit(solution)/shard_map/dot_general | solution.py:127
  43.6 3.4 %collective-permute-start.4 = (bf16[64,3584]{1,0:T(8,128)(2,1)S(1)}, bf16[64,3584]{1,0:T(8,128)(2,1)}, u32[]{:S(2)}, u32[]{:S(2)}) collective-permute-start(bf16[64,3584]{1,0:T(8,128)(2,1)S(1)} %collective-permute-done), channel_id=1, source_target_pairs={{0,1},{1,0},{2,3},{3,2},{4,5},{5,4},{6,7},{7,6},{8,9},{9,8},{10,11... | collective-permute-start | bytes 1376264 | tf_op jit(solution)/shard_map/ppermute | solution.py:21
  47.0 10.3 %all-to-all-done.1 = bf16[16,24,896]{2,1,0:T(8,128)(2,1)S(1)} async-done(((bf16[16,24,896]{2,1,0:T(8,128)(2,1)}), bf16[16,24,896]{2,1,0:T(8,128)(2,1)S(1)}, u32[]{:S(2)}, u32[]{:S(2)}) %all-to-all-start.1) | async-done | bytes 688160 | tf_op jit(solution)/shard_map/all_to_all | solution.py:88
  57.3 7.4 %all-to-all-start = ((bf16[16,24,896]{2,1,0:T(8,128)(2,1)}), bf16[16,24,896]{2,1,0:T(8,128)(2,1)S(1)}, u32[]{:S(2)}, u32[]{:S(2)}) async-start(bf16[16,24,896]{2,1,0:T(8,128)(2,1)} %bitcast.9), calls=%async_computation | async-start | bytes 1376256 | tf_op jit(solution)/shard_map/all_to_all | solution.py:88
  64.7 0.4 reshape.267
  65.2 0.0 collective-permute-done.2
  65.2 0.3 convolution_convert_fusion
  65.5 1.9 %collective-permute-start.3 = (bf16[48,3584]{1,0:T(8,128)(2,1)S(1)}, bf16[48,3584]{1,0:T(8,128)(2,1)S(1)}, u32[]{:S(2)}, u32[]{:S(2)}) collective-permute-start(bf16[48,3584]{1,0:T(8,128)(2,1)S(1)} %convolution_convert_fusion), channel_id=1, source_target_pairs={{0,2},{2,0},{4,6},{6,4},{8,10},{10,8},{12,14},{14,12},{16,18},{18,... | collective-permute-start | bytes 1032200 | tf_op jit(solution)/shard_map/ppermute | solution.py:21
  67.4 0.0 collective-permute-done.4
  67.4 1.1 %broadcast_select_fusion.3 = (bf16[64,3584]{1,0:T(8,128)(2,1)S(1)}, bf16[64,3584]{1,0:T(8,128)(2,1)S(1)}) fusion(bf16[64,3584]{1,0:T(8,128)(2,1)S(1)} %collective-permute-done, bf16[64,3584]{1,0:T(8,128)(2,1)} %collective-permute-done.4, pred[]{:T(512)S(6)} %eq.160), kind=kLoop, calls=%fused_computation.38 | loop fusion | flops 458752 | bytes 1835009 | tf_op jit(solution)/shard_map/jit(_where)/select_n | solution.py:150
  68.5 3.3 %fusion.13 = bf16[1,128,512]{2,1,0:T(8,128)(2,1)S(1)} fusion(bf16[1,512,3584]{2,1,0:T(8,128)(2,1)} %param.9, bf16[64,3584]{1,0:T(8,128)(2,1)S(1)} %get-tuple-element.29, bf16[64,3584]{1,0:T(8,128)(2,1)S(1)} %get-tuple-element.28), kind=kOutput, calls=%fused_computation.11 | convolution fusion | flops 471662592 | bytes 4718592 | tf_op jit(solution)/shard_map/td,hd->th/dot_general | solution.py:153
  71.8 3.4 %collective-permute-start.5 = (bf16[64,3584]{1,0:T(8,128)(2,1)S(1)}, bf16[64,3584]{1,0:T(8,128)(2,1)S(1)}, u32[]{:S(2)}, u32[]{:S(2)}) collective-permute-start(bf16[64,3584]{1,0:T(8,128)(2,1)S(1)} %collective-permute-done.2), channel_id=1, source_target_pairs={{0,1},{1,0},{2,3},{3,2},{4,5},{5,4},{6,7},{7,6},{8,9},{9,8},{10,11... | collective-permute-start | bytes 1376264 | tf_op jit(solution)/shard_map/ppermute | solution.py:21
  75.3 0.0 collective-permute-done.3
  75.3 0.3 fusion.36
  75.6 0.0 copy-start.3
  75.6 1.1 %fusion.31 = bf16[1,64,3584]{2,1,0:T(8,128)(2,1)} fusion(bf16[64,3584]{1,0:T(8,128)(2,1)S(1)} %collective-permute-done.2, f32[64,3584]{1,0:T(8,128)S(1)} %fusion.36, bf16[96,3584]{1,0:T(8,128)(2,1)S(1)} %reshape.267, s32[64]{0:T(128)S(1)} %get-tuple-element.23), kind=kOutput, calls=%fused_computation.32 | convolution fusion | flops 44963840 | bytes 2523392 | tf_op jit(solution)/shard_map/dot_general | solution.py:140
  76.7 10.0 %collective-permute-done.5 = bf16[64,3584]{1,0:T(8,128)(2,1)S(1)} collective-permute-done((bf16[64,3584]{1,0:T(8,128)(2,1)S(1)}, bf16[64,3584]{1,0:T(8,128)(2,1)S(1)}, u32[]{:S(2)}, u32[]{:S(2)}) %collective-permute-start.5) | collective-permute-done | bytes 458784 | tf_op jit(solution)/shard_map/ppermute | solution.py:21
  86.7 0.1 broadcast_select_fusion.1
  86.7 0.0 copy-done.3
  86.7 1.3 %fusion.10 = bf16[1,128,512]{2,1,0:T(8,128)(2,1)S(1)} fusion(bf16[1,512,3584]{2,1,0:T(8,128)(2,1)S(1)} %copy-done.3, bf16[64,3584]{1,0:T(8,128)(2,1)S(1)} %get-tuple-element.31, bf16[64,3584]{1,0:T(8,128)(2,1)S(1)} %get-tuple-element.30), kind=kOutput, calls=%fused_computation.10 | convolution fusion | flops 471662592 | bytes 4718592 | tf_op jit(solution)/shard_map/td,hd->th/dot_general | solution.py:153
  88.0 0.7 maximum_bitcast_fusion
  88.8 11.0 %all-to-all-done = bf16[16,24,896]{2,1,0:T(8,128)(2,1)S(1)} async-done(((bf16[16,24,896]{2,1,0:T(8,128)(2,1)}), bf16[16,24,896]{2,1,0:T(8,128)(2,1)S(1)}, u32[]{:S(2)}, u32[]{:S(2)}) %all-to-all-start) | async-done | bytes 688160 | tf_op jit(solution)/shard_map/all_to_all | solution.py:88
  99.8 1.1 %shard_map.76 = bf16[96,3584]{1,0:T(8,128)(2,1)} custom-call(bf16[384,896]{1,0:T(8,128)(2,1)S(1)} %bitcast.75), custom_call_target="tpu_custom_call" | custom-call | flops 88080384 | bytes 1376256 | tf_op jit(solution)/shard_map/pallas_call | solution.py:60
  (18 shorter events, 0.3 us)
Async XLA Ops:
  1.9 20.5 %copy-start = (bf16[2,1,64,3584]{3,2,1,0:T(8,128)(2,1)S(1)}, bf16[2,1,64,3584]{3,2,1,0:T(8,128)(2,1)}, u32[]{:S(2)}) copy-start(bf16[2,1,64,3584]{3,2,1,0:T(8,128)(2,1)} %param.5) | copy-start | bytes 2752516
  3.3 24.8 %copy-start.1 = (s32[2,1,64,1]{2,3,1,0:T(1,128)S(1)}, s32[2,1,64,1]{2,3,1,0:T(1,128)}, u32[]{:S(2)}) copy-start(s32[2,1,64,1]{2,3,1,0:T(1,128)} %param.6) | copy-start | bytes 1540
  3.3 34.5 %copy-start.2 = (f32[1,64]{1,0:T(1,128)S(1)}, f32[1,64]{1,0:T(1,128)}, u32[]{:S(2)}) copy-start(f32[1,64]{1,0:T(1,128)} %param.7) | copy-start | bytes 772
  3.3 54.0 %all-to-all-start.1 = ((bf16[16,24,896]{2,1,0:T(8,128)(2,1)}), bf16[16,24,896]{2,1,0:T(8,128)(2,1)S(1)}, u32[]{:S(2)}, u32[]{:S(2)}) async-start(bf16[16,24,896]{2,1,0:T(8,128)(2,1)} %bitcast.3), calls=%async_computation.1 | async-start | bytes 1376256 | tf_op jit(solution)/shard_map/all_to_all | solution.py:88
  22.4 15.4 %collective-permute-start = (bf16[64,3584]{1,0:T(8,128)(2,1)S(1)}, bf16[64,3584]{1,0:T(8,128)(2,1)S(1)}, u32[]{:S(2)}, u32[]{:S(2)}) collective-permute-start(bf16[64,3584]{1,0:T(8,128)(2,1)S(1)} %get-tuple-element.32), channel_id=1, source_target_pairs={{64,0},{128,64},{192,128},{256,192},{320,256},{384,320},{448,384},... | collective-permute-start | bytes 1376264 | tf_op jit(solution)/shard_map/ppermute | solution.py:16
  38.0 3.9 %collective-permute-start.1 = (bf16[72,3584]{1,0:T(8,128)(2,1)S(1)}, bf16[72,3584]{1,0:T(8,128)(2,1)S(1)}, u32[]{:S(2)}, u32[]{:S(2)}) collective-permute-start(bf16[72,3584]{1,0:T(8,128)(2,1)S(1)} %fusion.30), channel_id=1, source_target_pairs={{0,2},{2,0},{4,6},{6,4},{8,10},{10,8},{12,14},{14,12},{16,18},{18,... | collective-permute-start | bytes 1548296 | tf_op jit(solution)/shard_map/ppermute | solution.py:21
  40.0 25.2 %collective-permute-start.2 = (bf16[64,3584]{1,0:T(8,128)(2,1)S(1)}, bf16[64,3584]{1,0:T(8,128)(2,1)S(1)}, u32[]{:S(2)}, u32[]{:S(2)}) collective-permute-start(bf16[64,3584]{1,0:T(8,128)(2,1)S(1)} %get-tuple-element.12), channel_id=1, source_target_pairs={{0,64},{64,128},{128,192},{192,256},{256,320},{320,384},{384,448},... | collective-permute-start | bytes 1376264 | tf_op jit(solution)/shard_map/ppermute | solution.py:16
  43.6 23.8 %collective-permute-start.4 = (bf16[64,3584]{1,0:T(8,128)(2,1)S(1)}, bf16[64,3584]{1,0:T(8,128)(2,1)}, u32[]{:S(2)}, u32[]{:S(2)}) collective-permute-start(bf16[64,3584]{1,0:T(8,128)(2,1)S(1)} %collective-permute-done), channel_id=1, source_target_pairs={{0,1},{1,0},{2,3},{3,2},{4,5},{5,4},{6,7},{7,6},{8,9},{9,8},{10,11... | collective-permute-start | bytes 1376264 | tf_op jit(solution)/shard_map/ppermute | solution.py:21
  57.3 42.5 %all-to-all-start = ((bf16[16,24,896]{2,1,0:T(8,128)(2,1)}), bf16[16,24,896]{2,1,0:T(8,128)(2,1)S(1)}, u32[]{:S(2)}, u32[]{:S(2)}) async-start(bf16[16,24,896]{2,1,0:T(8,128)(2,1)} %bitcast.9), calls=%async_computation | async-start | bytes 1376256 | tf_op jit(solution)/shard_map/all_to_all | solution.py:88
  65.5 9.8 %collective-permute-start.3 = (bf16[48,3584]{1,0:T(8,128)(2,1)S(1)}, bf16[48,3584]{1,0:T(8,128)(2,1)S(1)}, u32[]{:S(2)}, u32[]{:S(2)}) collective-permute-start(bf16[48,3584]{1,0:T(8,128)(2,1)S(1)} %convolution_convert_fusion), channel_id=1, source_target_pairs={{0,2},{2,0},{4,6},{6,4},{8,10},{10,8},{12,14},{14,12},{16,18},{18,... | collective-permute-start | bytes 1032200 | tf_op jit(solution)/shard_map/ppermute | solution.py:21
  71.8 14.8 %collective-permute-start.5 = (bf16[64,3584]{1,0:T(8,128)(2,1)S(1)}, bf16[64,3584]{1,0:T(8,128)(2,1)S(1)}, u32[]{:S(2)}, u32[]{:S(2)}) collective-permute-start(bf16[64,3584]{1,0:T(8,128)(2,1)S(1)} %collective-permute-done.2), channel_id=1, source_target_pairs={{0,1},{1,0},{2,3},{3,2},{4,5},{5,4},{6,7},{7,6},{8,9},{9,8},{10,11... | collective-permute-start | bytes 1376264 | tf_op jit(solution)/shard_map/ppermute | solution.py:21
  75.6 11.1 %copy-start.3 = (bf16[1,512,3584]{2,1,0:T(8,128)(2,1)S(1)}, bf16[1,512,3584]{2,1,0:T(8,128)(2,1)}, u32[]{:S(2)}) copy-start(bf16[1,512,3584]{2,1,0:T(8,128)(2,1)} %param.9) | copy-start | bytes 11010052

commit v6 on v4

--- a/solution.py
+++ b/solution.py
@@ -31,6 +31,55 @@
 
 def select(rows, width, dtype=jnp.bfloat16):
     return (rows[:, None] == jnp.arange(width, dtype=jnp.int32)[None, :]).astype(dtype)
+
+
+def into_lines(rows):
+    count, width = rows.shape
+    part = width // PARTS
+    chunks, block = count // CHUNK, CHUNK * PARTS
+
+    def kernel(rows_ref, lines_ref, held, result, in_sem, out_sem):
+        arriving = [
+            pltpu.make_async_copy(rows_ref.at[pl.ds(q * CHUNK, CHUNK)], held.at[q], in_sem.at[q])
+            for q in range(chunks)
+        ]
+        for copy in arriving:
+            copy.start()
+        line = lax.broadcasted_iota(jnp.int32, (block, block), 0)
+        column = lax.broadcasted_iota(jnp.int32, (block, block), 1)
+        table = (column == (line % PARTS) * CHUNK + line // PARTS).astype(jnp.bfloat16)
+        leaving = []
+        for q in range(chunks):
+            arriving[q].wait()
+            stacked = jnp.concatenate(
+                [held[q, :, g * part : (g + 1) * part] for g in range(PARTS)], axis=0
+            )
+            moved = jnp.dot(table, stacked, preferred_element_type=jnp.float32)
+            result[q] = moved.astype(jnp.bfloat16)
+            copy = pltpu.make_async_copy(
+                result.at[q], lines_ref.at[pl.ds(q * block, block)], out_sem.at[q]
+            )
+            copy.start()
+            leaving.append(copy)
+        for copy in leaving:
+            copy.wait()
+
+    return pl.pallas_call(
+        kernel,
+        out_shape=jax.ShapeDtypeStruct((count * PARTS, part), rows.dtype),
+        in_specs=[pl.BlockSpec(memory_space=pl.ANY)],
+        out_specs=pl.BlockSpec(memory_space=pl.ANY),
+        scratch_shapes=[
+            pltpu.VMEM((chunks, CHUNK, width), rows.dtype),
+            pltpu.VMEM((chunks, block, part), rows.dtype),
+            pltpu.SemaphoreType.DMA((chunks,)),
+            pltpu.SemaphoreType.DMA((chunks,)),
+        ],
+        compiler_params=pltpu.CompilerParams(vmem_limit_bytes=60 << 20),
+        cost_estimate=pl.CostEstimate(
+            flops=2 * count * width * block, bytes_accessed=4 * count * width, transcendentals=0
+        ),
+    )(rows)
 
 
 def from_lines(lines):
@@ -89,7 +138,7 @@
             pieces, "expert", split_axis=0, concat_axis=0, tiled=True, axis_index_groups=across
         )
 
-    pieces = back_rows[0, 0, 0].reshape(chips, chip_rows * PARTS, part)
+    pieces = into_lines(back_rows[0, 0, 0]).reshape(chips, chip_rows * PARTS, part)
     pieces, grads = lax.optimization_barrier((pieces, grad_in))
     own_a = grads[0, 0]
     came = exchanged(pieces)

time: 101 us -> 101 us (level)
  Pallas kernels: 1.08 us -> 3.42 us
  local copies, waits for them, and re-layouts: 4.06 us -> 1.78 us
    pallas_call x0 -> x1, Pallas kernels: none -> 2.34 us  [into_lines(): pl.pallas_call(kernel, out_shape=jax.ShapeDtypeStruct((count * PARTS, par...]
    another operation x1 -> x0, local copies, waits for them, and re-layouts: 2.28 us -> none  [on_device(): pieces = back_rows[0, 0, 0].reshape(chips, chip_rows * PARTS, part)]
where the time goes in v6:
time: 101 us; the launch traced here: 100 us
  starting transfers between devices  44.9 us (44%)
  waiting for transfers between devices  39.1 us (39%)
  matrix products  7.78 us (8%)
  Pallas kernels  3.42 us (3%)
  other arithmetic  2.57 us (3%)
  local copies, waits for them, and re-layouts  1.78 us (2%)
    all_to_all x2, starting transfers between devices, exchanged(): lax.all_to_all(pieces, 'expert', split_axis=0, concat_axis=0, tiled=True,...  26.3 us
    all_to_all x2, waiting for transfers between devices, exchanged(): lax.all_to_all(pieces, 'expert', split_axis=0, concat_axis=0, tiled=True,...  19.9 us
    ppermute x4, starting transfers between devices, swapped(): return lax.ppermute(array, axis, [(i, i ^ 1) for i in range(peers)])  10.9 us
    ppermute x4, waiting for transfers between devices, swapped(): return lax.ppermute(array, axis, [(i, i ^ 1) for i in range(peers)])  9.96 us
    ppermute x2, waiting for transfers between devices, shifted(): return lax.ppermute(array, axis, pairs)  9.23 us
    ppermute x2, starting transfers between devices, shifted(): return lax.ppermute(array, axis, pairs)  7.64 us
    dot_general x2, matrix products, hidden(): jnp.einsum('td,hd->th', tokens, down_part, preferred_element_type=jnp.flo...  4.62 us
    pallas_call x1, Pallas kernels, into_lines(): pl.pallas_call(kernel, out_shape=jax.ShapeDtypeStruct((count * PARTS, par...  2.34 us
  transfers between devices with their start and end apart: 8, of which 4 were waited for; matrix products, arithmetic and copies ran while one was open for 12% of the time, Pallas kernels for 0%

profile of v6, /device:TPU:56, one launch (start us, length us, event | category | flops | bytes accessed | tf_op | source)
XLA Modules:
  0.0 100.4 jit_solution(3542589674787704851)
XLA Ops:
  0.6 0.0 copy-start
  0.6 0.0 copy-start.1
  0.7 2.3 %shard_map.76 = bf16[384,896]{1,0:T(8,128)(2,1)} custom-call(bf16[96,3584]{1,0:T(8,128)(2,1)} %bitcast.77), custom_call_target="tpu_custom_call" | custom-call | flops 88080384 | bytes 1376256 | tf_op jit(solution)/shard_map/pallas_call | solution.py:67
  3.0 18.9 %all-to-all-start.1 = ((bf16[16,24,896]{2,1,0:T(8,128)(2,1)}), bf16[16,24,896]{2,1,0:T(8,128)(2,1)S(1)}, u32[]{:S(2)}, u32[]{:S(2)}) async-start(bf16[16,24,896]{2,1,0:T(8,128)(2,1)} %bitcast.76), calls=%async_computation.1 | async-start | bytes 1376256 | tf_op jit(solution)/shard_map/all_to_all | solution.py:137
  21.9 1.2 %slice_bitcast_fusion = (bf16[64,3584]{1,0:T(8,128)(2,1)S(1)}, bf16[64,3584]{1,0:T(8,128)(2,1)S(1)}) fusion(bf16[2,1,64,3584]{3,2,1,0:T(8,128)(2,1)} %param.5), kind=kLoop, calls=%fused_computation.24 | loop fusion | bytes 1835008 | tf_op jit(solution)/shard_map/squeeze | solution.py:143
  23.1 5.7 %collective-permute-start = (bf16[64,3584]{1,0:T(8,128)(2,1)S(1)}, bf16[64,3584]{1,0:T(8,128)(2,1)S(1)}, u32[]{:S(2)}, u32[]{:S(2)}) collective-permute-start(bf16[64,3584]{1,0:T(8,128)(2,1)S(1)} %get-tuple-element.32), channel_id=1, source_target_pairs={{64,0},{128,64},{192,128},{256,192},{320,256},{384,320},{448,384},... | collective-permute-start | bytes 1376264 | tf_op jit(solution)/shard_map/ppermute | solution.py:16
  28.8 0.0 copy-done
  28.9 0.2 convert_reduce_fusion
  29.0 0.2 convert_reduce_fusion.1
  29.3 9.2 %collective-permute-done = bf16[64,3584]{1,0:T(8,128)(2,1)S(1)} collective-permute-done((bf16[64,3584]{1,0:T(8,128)(2,1)S(1)}, bf16[64,3584]{1,0:T(8,128)(2,1)S(1)}, u32[]{:S(2)}, u32[]{:S(2)}) %collective-permute-start) | collective-permute-done | bytes 458784 | tf_op jit(solution)/shard_map/ppermute | solution.py:16
  38.5 0.0 copy-done.1
  38.5 0.1 multiply_convert_fusion
  38.7 1.9 %collective-permute-start.1 = (bf16[72,3584]{1,0:T(8,128)(2,1)S(1)}, bf16[72,3584]{1,0:T(8,128)(2,1)S(1)}, u32[]{:S(2)}, u32[]{:S(2)}) collective-permute-start(bf16[72,3584]{1,0:T(8,128)(2,1)S(1)} %fusion.23), channel_id=1, source_target_pairs={{0,2},{2,0},{4,6},{6,4},{8,10},{10,8},{12,14},{14,12},{16,18},{18,... | collective-permute-start | bytes 1548296 | tf_op jit(solution)/shard_map/ppermute | solution.py:21
  40.6 1.9 %collective-permute-start.2 = (bf16[64,3584]{1,0:T(8,128)(2,1)S(1)}, bf16[64,3584]{1,0:T(8,128)(2,1)S(1)}, u32[]{:S(2)}, u32[]{:S(2)}) collective-permute-start(bf16[64,3584]{1,0:T(8,128)(2,1)S(1)} %get-tuple-element.12), channel_id=1, source_target_pairs={{0,64},{64,128},{128,192},{192,256},{256,320},{320,384},{384,448},... | collective-permute-start | bytes 1376264 | tf_op jit(solution)/shard_map/ppermute | solution.py:16
  42.6 0.0 collective-permute-done.1
  42.6 0.1 broadcast_add_fusion.2
  42.9 1.4 %convolution_convert_fusion.1 = bf16[384,896]{1,0:T(8,128)(2,1)} fusion(bf16[512,896]{1,0:T(8,128)(2,1)S(1)} %slice_dynamic-update-slice_fusion, s32[512]{0:T(512)S(1)} %pad_add_fusion), kind=kOutput, calls=%fused_computation.6 | convolution fusion | flops 352862208 | bytes 1607680 | tf_op jit(solution)/shard_map/dot_general | solution.py:170
  44.3 3.4 %collective-permute-start.4 = (bf16[64,3584]{1,0:T(8,128)(2,1)S(1)}, bf16[64,3584]{1,0:T(8,128)(2,1)}, u32[]{:S(2)}, u32[]{:S(2)}) collective-permute-start(bf16[64,3584]{1,0:T(8,128)(2,1)S(1)} %collective-permute-done), channel_id=1, source_target_pairs={{0,1},{1,0},{2,3},{3,2},{4,5},{5,4},{6,7},{7,6},{8,9},{9,8},{10,11... | collective-permute-start | bytes 1376264 | tf_op jit(solution)/shard_map/ppermute | solution.py:21
  47.7 9.1 %all-to-all-done.1 = bf16[16,24,896]{2,1,0:T(8,128)(2,1)S(1)} async-done(((bf16[16,24,896]{2,1,0:T(8,128)(2,1)}), bf16[16,24,896]{2,1,0:T(8,128)(2,1)S(1)}, u32[]{:S(2)}, u32[]{:S(2)}) %all-to-all-start.1) | async-done | bytes 688160 | tf_op jit(solution)/shard_map/all_to_all | solution.py:137
  56.8 7.5 %all-to-all-start = ((bf16[16,24,896]{2,1,0:T(8,128)(2,1)}), bf16[16,24,896]{2,1,0:T(8,128)(2,1)S(1)}, u32[]{:S(2)}, u32[]{:S(2)}) async-start(bf16[16,24,896]{2,1,0:T(8,128)(2,1)} %bitcast.9), calls=%async_computation | async-start | bytes 1376256 | tf_op jit(solution)/shard_map/all_to_all | solution.py:137
  64.3 0.4 reshape.245
  64.7 0.0 collective-permute-done.2
  64.7 0.3 convolution_convert_fusion
  65.0 1.9 %collective-permute-start.3 = (bf16[48,3584]{1,0:T(8,128)(2,1)S(1)}, bf16[48,3584]{1,0:T(8,128)(2,1)S(1)}, u32[]{:S(2)}, u32[]{:S(2)}) collective-permute-start(bf16[48,3584]{1,0:T(8,128)(2,1)S(1)} %convolution_convert_fusion), channel_id=1, source_target_pairs={{0,2},{2,0},{4,6},{6,4},{8,10},{10,8},{12,14},{14,12},{16,18},{18,... | collective-permute-start | bytes 1032200 | tf_op jit(solution)/shard_map/ppermute | solution.py:21
  67.0 0.0 collective-permute-done.4
  67.0 1.1 %broadcast_select_fusion.3 = (bf16[64,3584]{1,0:T(8,128)(2,1)S(1)}, bf16[64,3584]{1,0:T(8,128)(2,1)S(1)}) fusion(bf16[64,3584]{1,0:T(8,128)(2,1)S(1)} %collective-permute-done, bf16[64,3584]{1,0:T(8,128)(2,1)} %collective-permute-done.4, pred[]{:T(512)S(6)} %eq.142), kind=kLoop, calls=%fused_computation.29 | loop fusion | flops 458752 | bytes 1835009 | tf_op jit(solution)/shard_map/jit(_where)/select_n | solution.py:193
  68.1 3.3 %fusion.13 = bf16[1,128,512]{2,1,0:T(8,128)(2,1)S(1)} fusion(bf16[1,512,3584]{2,1,0:T(8,128)(2,1)} %param.9, bf16[64,3584]{1,0:T(8,128)(2,1)S(1)} %get-tuple-element.29, bf16[64,3584]{1,0:T(8,128)(2,1)S(1)} %get-tuple-element.28), kind=kOutput, calls=%fused_computation.10 | convolution fusion | flops 471662592 | bytes 4718592 | tf_op jit(solution)/shard_map/td,hd->th/dot_general | solution.py:196
  71.4 0.0 copy-start.2
  71.4 3.7 %collective-permute-start.5 = (bf16[64,3584]{1,0:T(8,128)(2,1)S(1)}, bf16[64,3584]{1,0:T(8,128)(2,1)S(1)}, u32[]{:S(2)}, u32[]{:S(2)}) collective-permute-start(bf16[64,3584]{1,0:T(8,128)(2,1)S(1)} %collective-permute-done.2), channel_id=1, source_target_pairs={{0,1},{1,0},{2,3},{3,2},{4,5},{5,4},{6,7},{7,6},{8,9},{9,8},{10,11... | collective-permute-start | bytes 1376264 | tf_op jit(solution)/shard_map/ppermute | solution.py:21
  75.1 0.0 collective-permute-done.3
  75.1 0.3 fusion.28
  75.4 1.1 %fusion.24 = bf16[1,64,3584]{2,1,0:T(8,128)(2,1)} fusion(bf16[64,3584]{1,0:T(8,128)(2,1)S(1)} %collective-permute-done.2, f32[64,3584]{1,0:T(8,128)S(1)} %fusion.28, bf16[96,3584]{1,0:T(8,128)(2,1)S(1)} %reshape.245, s32[64]{0:T(128)S(1)} %get-tuple-element.23), kind=kOutput, calls=%fused_computation.23 | convolution fusion | flops 44963840 | bytes 2523392 | tf_op jit(solution)/shard_map/dot_general | solution.py:183
  76.5 10.0 %collective-permute-done.5 = bf16[64,3584]{1,0:T(8,128)(2,1)S(1)} collective-permute-done((bf16[64,3584]{1,0:T(8,128)(2,1)S(1)}, bf16[64,3584]{1,0:T(8,128)(2,1)S(1)}, u32[]{:S(2)}, u32[]{:S(2)}) %collective-permute-start.5) | collective-permute-done | bytes 458784 | tf_op jit(solution)/shard_map/ppermute | solution.py:21
  86.5 0.1 broadcast_select_fusion.1
  86.6 0.0 copy-done.2
  86.6 1.3 %fusion.10 = bf16[1,128,512]{2,1,0:T(8,128)(2,1)S(1)} fusion(bf16[1,512,3584]{2,1,0:T(8,128)(2,1)S(1)} %copy-done.2, bf16[64,3584]{1,0:T(8,128)(2,1)S(1)} %get-tuple-element.31, bf16[64,3584]{1,0:T(8,128)(2,1)S(1)} %get-tuple-element.30), kind=kOutput, calls=%fused_computation.9 | convolution fusion | flops 471662592 | bytes 4718592 | tf_op jit(solution)/shard_map/td,hd->th/dot_general | solution.py:196
  87.9 0.7 maximum_bitcast_fusion
  88.6 10.7 %all-to-all-done = bf16[16,24,896]{2,1,0:T(8,128)(2,1)S(1)} async-done(((bf16[16,24,896]{2,1,0:T(8,128)(2,1)}), bf16[16,24,896]{2,1,0:T(8,128)(2,1)S(1)}, u32[]{:S(2)}, u32[]{:S(2)}) %all-to-all-start) | async-done | bytes 688160 | tf_op jit(solution)/shard_map/all_to_all | solution.py:137
  99.3 1.1 %shard_map.77 = bf16[96,3584]{1,0:T(8,128)(2,1)} custom-call(bf16[384,896]{1,0:T(8,128)(2,1)S(1)} %bitcast.75), custom_call_target="tpu_custom_call" | custom-call | flops 88080384 | bytes 1376256 | tf_op jit(solution)/shard_map/pallas_call | solution.py:109
  (17 shorter events, 0.3 us)
Async XLA Ops:
  0.6 28.2 %copy-start = (s32[2,1,64,1]{2,3,1,0:T(1,128)S(1)}, s32[2,1,64,1]{2,3,1,0:T(1,128)}, u32[]{:S(2)}) copy-start(s32[2,1,64,1]{2,3,1,0:T(1,128)} %param.6) | copy-start | bytes 1540
  0.6 37.8 %copy-start.1 = (f32[1,64]{1,0:T(1,128)S(1)}, f32[1,64]{1,0:T(1,128)}, u32[]{:S(2)}) copy-start(f32[1,64]{1,0:T(1,128)} %param.7) | copy-start | bytes 772
  3.0 53.8 %all-to-all-start.1 = ((bf16[16,24,896]{2,1,0:T(8,128)(2,1)}), bf16[16,24,896]{2,1,0:T(8,128)(2,1)S(1)}, u32[]{:S(2)}, u32[]{:S(2)}) async-start(bf16[16,24,896]{2,1,0:T(8,128)(2,1)} %bitcast.76), calls=%async_computation.1 | async-start | bytes 1376256 | tf_op jit(solution)/shard_map/all_to_all | solution.py:137
  23.1 15.4 %collective-permute-start = (bf16[64,3584]{1,0:T(8,128)(2,1)S(1)}, bf16[64,3584]{1,0:T(8,128)(2,1)S(1)}, u32[]{:S(2)}, u32[]{:S(2)}) collective-permute-start(bf16[64,3584]{1,0:T(8,128)(2,1)S(1)} %get-tuple-element.32), channel_id=1, source_target_pairs={{64,0},{128,64},{192,128},{256,192},{320,256},{384,320},{448,384},... | collective-permute-start | bytes 1376264 | tf_op jit(solution)/shard_map/ppermute | solution.py:16
  38.7 3.9 %collective-permute-start.1 = (bf16[72,3584]{1,0:T(8,128)(2,1)S(1)}, bf16[72,3584]{1,0:T(8,128)(2,1)S(1)}, u32[]{:S(2)}, u32[]{:S(2)}) collective-permute-start(bf16[72,3584]{1,0:T(8,128)(2,1)S(1)} %fusion.23), channel_id=1, source_target_pairs={{0,2},{2,0},{4,6},{6,4},{8,10},{10,8},{12,14},{14,12},{16,18},{18,... | collective-permute-start | bytes 1548296 | tf_op jit(solution)/shard_map/ppermute | solution.py:21
  40.6 24.1 %collective-permute-start.2 = (bf16[64,3584]{1,0:T(8,128)(2,1)S(1)}, bf16[64,3584]{1,0:T(8,128)(2,1)S(1)}, u32[]{:S(2)}, u32[]{:S(2)}) collective-permute-start(bf16[64,3584]{1,0:T(8,128)(2,1)S(1)} %get-tuple-element.12), channel_id=1, source_target_pairs={{0,64},{64,128},{128,192},{192,256},{256,320},{320,384},{384,448},... | collective-permute-start | bytes 1376264 | tf_op jit(solution)/shard_map/ppermute | solution.py:16
  44.3 22.7 %collective-permute-start.4 = (bf16[64,3584]{1,0:T(8,128)(2,1)S(1)}, bf16[64,3584]{1,0:T(8,128)(2,1)}, u32[]{:S(2)}, u32[]{:S(2)}) collective-permute-start(bf16[64,3584]{1,0:T(8,128)(2,1)S(1)} %collective-permute-done), channel_id=1, source_target_pairs={{0,1},{1,0},{2,3},{3,2},{4,5},{5,4},{6,7},{7,6},{8,9},{9,8},{10,11... | collective-permute-start | bytes 1376264 | tf_op jit(solution)/shard_map/ppermute | solution.py:21
  56.8 42.5 %all-to-all-start = ((bf16[16,24,896]{2,1,0:T(8,128)(2,1)}), bf16[16,24,896]{2,1,0:T(8,128)(2,1)S(1)}, u32[]{:S(2)}, u32[]{:S(2)}) async-start(bf16[16,24,896]{2,1,0:T(8,128)(2,1)} %bitcast.9), calls=%async_computation | async-start | bytes 1376256 | tf_op jit(solution)/shard_map/all_to_all | solution.py:137
  65.0 10.1 %collective-permute-start.3 = (bf16[48,3584]{1,0:T(8,128)(2,1)S(1)}, bf16[48,3584]{1,0:T(8,128)(2,1)S(1)}, u32[]{:S(2)}, u32[]{:S(2)}) collective-permute-start(bf16[48,3584]{1,0:T(8,128)(2,1)S(1)} %convolution_convert_fusion), channel_id=1, source_target_pairs={{0,2},{2,0},{4,6},{6,4},{8,10},{10,8},{12,14},{14,12},{16,18},{18,... | collective-permute-start | bytes 1032200 | tf_op jit(solution)/shard_map/ppermute | solution.py:21
  71.4 15.2 %copy-start.2 = (bf16[1,512,3584]{2,1,0:T(8,128)(2,1)S(1)}, bf16[1,512,3584]{2,1,0:T(8,128)(2,1)}, u32[]{:S(2)}) copy-start(bf16[1,512,3584]{2,1,0:T(8,128)(2,1)} %param.9) | copy-start | bytes 11010052
  71.4 15.1 %collective-permute-start.5 = (bf16[64,3584]{1,0:T(8,128)(2,1)S(1)}, bf16[64,3584]{1,0:T(8,128)(2,1)S(1)}, u32[]{:S(2)}, u32[]{:S(2)}) collective-permute-start(bf16[64,3584]{1,0:T(8,128)(2,1)S(1)} %collective-permute-done.2), channel_id=1, source_target_pairs={{0,1},{1,0},{2,3},{3,2},{4,5},{5,4},{6,7},{7,6},{8,9},{9,8},{10,11... | collective-permute-start | bytes 1376264 | tf_op jit(solution)/shard_map/ppermute | solution.py:21

commit v7 on v4

--- a/solution.py
+++ b/solution.py
@@ -7,7 +7,7 @@
 
 CORES = 2
 PARTS = 4
-CHUNK = 32
+CHUNK = 48
 
 
 def shifted(array, axis, by):

time: 101 us -> 101 us (level)
  no operation moved by 1% of the time
where the time goes in v7:
time: 101 us; the launch traced here: 100 us
  starting transfers between devices  44.8 us (44%)
  waiting for transfers between devices  39.1 us (39%)
  matrix products  7.77 us (8%)
  local copies, waits for them, and re-layouts  4.06 us (4%)
  other arithmetic  2.57 us (3%)
  Pallas kernels  1.11 us (1%)
    all_to_all x2, starting transfers between devices, exchanged(): lax.all_to_all(pieces, 'expert', split_axis=0, concat_axis=0, tiled=True,...  26.3 us
    all_to_all x2, waiting for transfers between devices, exchanged(): lax.all_to_all(pieces, 'expert', split_axis=0, concat_axis=0, tiled=True,...  19.9 us
    ppermute x4, starting transfers between devices, swapped(): return lax.ppermute(array, axis, [(i, i ^ 1) for i in range(peers)])  10.9 us
    ppermute x4, waiting for transfers between devices, swapped(): return lax.ppermute(array, axis, [(i, i ^ 1) for i in range(peers)])  9.97 us
    ppermute x2, waiting for transfers between devices, shifted(): return lax.ppermute(array, axis, pairs)  9.23 us
    ppermute x2, starting transfers between devices, shifted(): return lax.ppermute(array, axis, pairs)  7.64 us
    dot_general x2, matrix products, hidden(): jnp.einsum('td,hd->th', tokens, down_part, preferred_element_type=jnp.flo...  4.63 us
    another operation x1, local copies, waits for them, and re-layouts, on_device(): pieces = back_rows[0, 0, 0].reshape(chips, chip_rows * PARTS, part)  2.28 us
  transfers between devices with their start and end apart: 8, of which 4 were waited for; matrix products, arithmetic and copies ran while one was open for 12% of the time, Pallas kernels for 0%

profile of v7, /device:TPU:56, one launch (start us, length us, event | category | flops | bytes accessed | tf_op | source)
XLA Modules:
  0.0 100.4 jit_solution(5751799355038496911)
XLA Ops:
  0.6 0.0 copy-start
  0.6 0.0 copy-start.1
  0.7 2.3 %reshape_squeeze.3 = bf16[16,24,896]{2,1,0:T(8,128)(2,1)} reshape(bf16[1,1,1,96,3584]{4,3,2,1,0:T(8,128)(2,1)} %param.8) | data formatting | bytes 1376256 | tf_op jit(solution)/shard_map/reshape;squeeze | solution.py:92
  2.9 18.9 %all-to-all-start.1 = ((bf16[16,24,896]{2,1,0:T(8,128)(2,1)}), bf16[16,24,896]{2,1,0:T(8,128)(2,1)S(1)}, u32[]{:S(2)}, u32[]{:S(2)}) async-start(bf16[16,24,896]{2,1,0:T(8,128)(2,1)} %reshape_squeeze.3), calls=%async_computation.1 | async-start | bytes 1376256 | tf_op jit(solution)/shard_map/all_to_all | solution.py:88
  21.8 1.2 %slice_bitcast_fusion = (bf16[64,3584]{1,0:T(8,128)(2,1)S(1)}, bf16[64,3584]{1,0:T(8,128)(2,1)S(1)}) fusion(bf16[2,1,64,3584]{3,2,1,0:T(8,128)(2,1)} %param.5), kind=kLoop, calls=%fused_computation.24 | loop fusion | bytes 1835008 | tf_op jit(solution)/shard_map/squeeze | solution.py:94
  23.0 5.7 %collective-permute-start = (bf16[64,3584]{1,0:T(8,128)(2,1)S(1)}, bf16[64,3584]{1,0:T(8,128)(2,1)S(1)}, u32[]{:S(2)}, u32[]{:S(2)}) collective-permute-start(bf16[64,3584]{1,0:T(8,128)(2,1)S(1)} %get-tuple-element.32), channel_id=1, source_target_pairs={{64,0},{128,64},{192,128},{256,192},{320,256},{384,320},{448,384},... | collective-permute-start | bytes 1376264 | tf_op jit(solution)/shard_map/ppermute | solution.py:16
  28.7 0.0 copy-done
  28.8 0.2 convert_reduce_fusion
  29.0 0.2 convert_reduce_fusion.1
  29.2 9.2 %collective-permute-done = bf16[64,3584]{1,0:T(8,128)(2,1)S(1)} collective-permute-done((bf16[64,3584]{1,0:T(8,128)(2,1)S(1)}, bf16[64,3584]{1,0:T(8,128)(2,1)S(1)}, u32[]{:S(2)}, u32[]{:S(2)}) %collective-permute-start) | collective-permute-done | bytes 458784 | tf_op jit(solution)/shard_map/ppermute | solution.py:16
  38.4 0.0 copy-done.1
  38.4 0.1 multiply_convert_fusion
  38.6 1.9 %collective-permute-start.1 = (bf16[72,3584]{1,0:T(8,128)(2,1)S(1)}, bf16[72,3584]{1,0:T(8,128)(2,1)S(1)}, u32[]{:S(2)}, u32[]{:S(2)}) collective-permute-start(bf16[72,3584]{1,0:T(8,128)(2,1)S(1)} %fusion.23), channel_id=1, source_target_pairs={{0,2},{2,0},{4,6},{6,4},{8,10},{10,8},{12,14},{14,12},{16,18},{18,... | collective-permute-start | bytes 1548296 | tf_op jit(solution)/shard_map/ppermute | solution.py:21
  40.6 1.9 %collective-permute-start.2 = (bf16[64,3584]{1,0:T(8,128)(2,1)S(1)}, bf16[64,3584]{1,0:T(8,128)(2,1)S(1)}, u32[]{:S(2)}, u32[]{:S(2)}) collective-permute-start(bf16[64,3584]{1,0:T(8,128)(2,1)S(1)} %get-tuple-element.12), channel_id=1, source_target_pairs={{0,64},{64,128},{128,192},{192,256},{256,320},{320,384},{384,448},... | collective-permute-start | bytes 1376264 | tf_op jit(solution)/shard_map/ppermute | solution.py:16
  42.5 0.0 collective-permute-done.1
  42.5 0.1 broadcast_add_fusion.2
  42.8 1.4 %convolution_convert_fusion.1 = bf16[384,896]{1,0:T(8,128)(2,1)} fusion(bf16[512,896]{1,0:T(8,128)(2,1)S(1)} %slice_dynamic-update-slice_fusion, s32[512]{0:T(512)S(1)} %pad_add_fusion), kind=kOutput, calls=%fused_computation.6 | convolution fusion | flops 352862208 | bytes 1607680 | tf_op jit(solution)/shard_map/dot_general | solution.py:121
  44.2 3.4 %collective-permute-start.4 = (bf16[64,3584]{1,0:T(8,128)(2,1)S(1)}, bf16[64,3584]{1,0:T(8,128)(2,1)}, u32[]{:S(2)}, u32[]{:S(2)}) collective-permute-start(bf16[64,3584]{1,0:T(8,128)(2,1)S(1)} %collective-permute-done), channel_id=1, source_target_pairs={{0,1},{1,0},{2,3},{3,2},{4,5},{5,4},{6,7},{7,6},{8,9},{9,8},{10,11... | collective-permute-start | bytes 1376264 | tf_op jit(solution)/shard_map/ppermute | solution.py:21
  47.6 9.1 %all-to-all-done.1 = bf16[16,24,896]{2,1,0:T(8,128)(2,1)S(1)} async-done(((bf16[16,24,896]{2,1,0:T(8,128)(2,1)}), bf16[16,24,896]{2,1,0:T(8,128)(2,1)S(1)}, u32[]{:S(2)}, u32[]{:S(2)}) %all-to-all-start.1) | async-done | bytes 688160 | tf_op jit(solution)/shard_map/all_to_all | solution.py:88
  56.8 7.4 %all-to-all-start = ((bf16[16,24,896]{2,1,0:T(8,128)(2,1)}), bf16[16,24,896]{2,1,0:T(8,128)(2,1)S(1)}, u32[]{:S(2)}, u32[]{:S(2)}) async-start(bf16[16,24,896]{2,1,0:T(8,128)(2,1)} %bitcast.7), calls=%async_computation | async-start | bytes 1376256 | tf_op jit(solution)/shard_map/all_to_all | solution.py:88
  64.2 0.4 reshape.241
  64.6 0.0 collective-permute-done.2
  64.6 0.3 convolution_convert_fusion
  64.9 1.9 %collective-permute-start.3 = (bf16[48,3584]{1,0:T(8,128)(2,1)S(1)}, bf16[48,3584]{1,0:T(8,128)(2,1)S(1)}, u32[]{:S(2)}, u32[]{:S(2)}) collective-permute-start(bf16[48,3584]{1,0:T(8,128)(2,1)S(1)} %convolution_convert_fusion), channel_id=1, source_target_pairs={{0,2},{2,0},{4,6},{6,4},{8,10},{10,8},{12,14},{14,12},{16,18},{18,... | collective-permute-start | bytes 1032200 | tf_op jit(solution)/shard_map/ppermute | solution.py:21
  66.9 0.0 collective-permute-done.4
  66.9 1.1 %broadcast_select_fusion.3 = (bf16[64,3584]{1,0:T(8,128)(2,1)S(1)}, bf16[64,3584]{1,0:T(8,128)(2,1)S(1)}) fusion(bf16[64,3584]{1,0:T(8,128)(2,1)S(1)} %collective-permute-done, bf16[64,3584]{1,0:T(8,128)(2,1)} %collective-permute-done.4, pred[]{:T(512)S(6)} %eq.142), kind=kLoop, calls=%fused_computation.29 | loop fusion | flops 458752 | bytes 1835009 | tf_op jit(solution)/shard_map/jit(_where)/select_n | solution.py:144
  68.0 3.3 %fusion.13 = bf16[1,128,512]{2,1,0:T(8,128)(2,1)S(1)} fusion(bf16[1,512,3584]{2,1,0:T(8,128)(2,1)} %param.9, bf16[64,3584]{1,0:T(8,128)(2,1)S(1)} %get-tuple-element.29, bf16[64,3584]{1,0:T(8,128)(2,1)S(1)} %get-tuple-element.28), kind=kOutput, calls=%fused_computation.10 | convolution fusion | flops 471662592 | bytes 4718592 | tf_op jit(solution)/shard_map/td,hd->th/dot_general | solution.py:147
  71.3 0.0 copy-start.2
  71.3 3.7 %collective-permute-start.5 = (bf16[64,3584]{1,0:T(8,128)(2,1)S(1)}, bf16[64,3584]{1,0:T(8,128)(2,1)S(1)}, u32[]{:S(2)}, u32[]{:S(2)}) collective-permute-start(bf16[64,3584]{1,0:T(8,128)(2,1)S(1)} %collective-permute-done.2), channel_id=1, source_target_pairs={{0,1},{1,0},{2,3},{3,2},{4,5},{5,4},{6,7},{7,6},{8,9},{9,8},{10,11... | collective-permute-start | bytes 1376264 | tf_op jit(solution)/shard_map/ppermute | solution.py:21
  75.0 0.0 collective-permute-done.3
  75.0 0.3 fusion.28
  75.3 1.1 %fusion.24 = bf16[1,64,3584]{2,1,0:T(8,128)(2,1)} fusion(bf16[64,3584]{1,0:T(8,128)(2,1)S(1)} %collective-permute-done.2, f32[64,3584]{1,0:T(8,128)S(1)} %fusion.28, bf16[96,3584]{1,0:T(8,128)(2,1)S(1)} %reshape.241, s32[64]{0:T(128)S(1)} %get-tuple-element.23), kind=kOutput, calls=%fused_computation.23 | convolution fusion | flops 44963840 | bytes 2523392 | tf_op jit(solution)/shard_map/dot_general | solution.py:134
  76.4 10.0 %collective-permute-done.5 = bf16[64,3584]{1,0:T(8,128)(2,1)S(1)} collective-permute-done((bf16[64,3584]{1,0:T(8,128)(2,1)S(1)}, bf16[64,3584]{1,0:T(8,128)(2,1)S(1)}, u32[]{:S(2)}, u32[]{:S(2)}) %collective-permute-start.5) | collective-permute-done | bytes 458784 | tf_op jit(solution)/shard_map/ppermute | solution.py:21
  86.4 0.1 broadcast_select_fusion.1
  86.5 0.0 copy-done.2
  86.5 1.3 %fusion.10 = bf16[1,128,512]{2,1,0:T(8,128)(2,1)S(1)} fusion(bf16[1,512,3584]{2,1,0:T(8,128)(2,1)S(1)} %copy-done.2, bf16[64,3584]{1,0:T(8,128)(2,1)S(1)} %get-tuple-element.31, bf16[64,3584]{1,0:T(8,128)(2,1)S(1)} %get-tuple-element.30), kind=kOutput, calls=%fused_computation.9 | convolution fusion | flops 471662592 | bytes 4718592 | tf_op jit(solution)/shard_map/td,hd->th/dot_general | solution.py:147
  87.8 0.7 maximum_bitcast_fusion
  88.5 10.7 %all-to-all-done = bf16[16,24,896]{2,1,0:T(8,128)(2,1)S(1)} async-done(((bf16[16,24,896]{2,1,0:T(8,128)(2,1)}), bf16[16,24,896]{2,1,0:T(8,128)(2,1)S(1)}, u32[]{:S(2)}, u32[]{:S(2)}) %all-to-all-start) | async-done | bytes 688160 | tf_op jit(solution)/shard_map/all_to_all | solution.py:88
  99.2 1.1 %shard_map.76 = bf16[96,3584]{1,0:T(8,128)(2,1)} custom-call(bf16[384,896]{1,0:T(8,128)(2,1)S(1)} %bitcast.75), custom_call_target="tpu_custom_call" | custom-call | flops 132120576 | bytes 1376256 | tf_op jit(solution)/shard_map/pallas_call | solution.py:60
  (17 shorter events, 0.3 us)
Async XLA Ops:
  0.6 28.1 %copy-start = (s32[2,1,64,1]{2,3,1,0:T(1,128)S(1)}, s32[2,1,64,1]{2,3,1,0:T(1,128)}, u32[]{:S(2)}) copy-start(s32[2,1,64,1]{2,3,1,0:T(1,128)} %param.6) | copy-start | bytes 1540
  0.6 37.8 %copy-start.1 = (f32[1,64]{1,0:T(1,128)S(1)}, f32[1,64]{1,0:T(1,128)}, u32[]{:S(2)}) copy-start(f32[1,64]{1,0:T(1,128)} %param.7) | copy-start | bytes 772
  2.9 53.8 %all-to-all-start.1 = ((bf16[16,24,896]{2,1,0:T(8,128)(2,1)}), bf16[16,24,896]{2,1,0:T(8,128)(2,1)S(1)}, u32[]{:S(2)}, u32[]{:S(2)}) async-start(bf16[16,24,896]{2,1,0:T(8,128)(2,1)} %reshape_squeeze.3), calls=%async_computation.1 | async-start | bytes 1376256 | tf_op jit(solution)/shard_map/all_to_all | solution.py:88
  23.0 15.4 %collective-permute-start = (bf16[64,3584]{1,0:T(8,128)(2,1)S(1)}, bf16[64,3584]{1,0:T(8,128)(2,1)S(1)}, u32[]{:S(2)}, u32[]{:S(2)}) collective-permute-start(bf16[64,3584]{1,0:T(8,128)(2,1)S(1)} %get-tuple-element.32), channel_id=1, source_target_pairs={{64,0},{128,64},{192,128},{256,192},{320,256},{384,320},{448,384},... | collective-permute-start | bytes 1376264 | tf_op jit(solution)/shard_map/ppermute | solution.py:16
  38.6 3.9 %collective-permute-start.1 = (bf16[72,3584]{1,0:T(8,128)(2,1)S(1)}, bf16[72,3584]{1,0:T(8,128)(2,1)S(1)}, u32[]{:S(2)}, u32[]{:S(2)}) collective-permute-start(bf16[72,3584]{1,0:T(8,128)(2,1)S(1)} %fusion.23), channel_id=1, source_target_pairs={{0,2},{2,0},{4,6},{6,4},{8,10},{10,8},{12,14},{14,12},{16,18},{18,... | collective-permute-start | bytes 1548296 | tf_op jit(solution)/shard_map/ppermute | solution.py:21
  40.6 24.1 %collective-permute-start.2 = (bf16[64,3584]{1,0:T(8,128)(2,1)S(1)}, bf16[64,3584]{1,0:T(8,128)(2,1)S(1)}, u32[]{:S(2)}, u32[]{:S(2)}) collective-permute-start(bf16[64,3584]{1,0:T(8,128)(2,1)S(1)} %get-tuple-element.12), channel_id=1, source_target_pairs={{0,64},{64,128},{128,192},{192,256},{256,320},{320,384},{384,448},... | collective-permute-start | bytes 1376264 | tf_op jit(solution)/shard_map/ppermute | solution.py:16
  44.2 22.7 %collective-permute-start.4 = (bf16[64,3584]{1,0:T(8,128)(2,1)S(1)}, bf16[64,3584]{1,0:T(8,128)(2,1)}, u32[]{:S(2)}, u32[]{:S(2)}) collective-permute-start(bf16[64,3584]{1,0:T(8,128)(2,1)S(1)} %collective-permute-done), channel_id=1, source_target_pairs={{0,1},{1,0},{2,3},{3,2},{4,5},{5,4},{6,7},{7,6},{8,9},{9,8},{10,11... | collective-permute-start | bytes 1376264 | tf_op jit(solution)/shard_map/ppermute | solution.py:21
  56.8 42.5 %all-to-all-start = ((bf16[16,24,896]{2,1,0:T(8,128)(2,1)}), bf16[16,24,896]{2,1,0:T(8,128)(2,1)S(1)}, u32[]{:S(2)}, u32[]{:S(2)}) async-start(bf16[16,24,896]{2,1,0:T(8,128)(2,1)} %bitcast.7), calls=%async_computation | async-start | bytes 1376256 | tf_op jit(solution)/shard_map/all_to_all | solution.py:88
  64.9 10.1 %collective-permute-start.3 = (bf16[48,3584]{1,0:T(8,128)(2,1)S(1)}, bf16[48,3584]{1,0:T(8,128)(2,1)S(1)}, u32[]{:S(2)}, u32[]{:S(2)}) collective-permute-start(bf16[48,3584]{1,0:T(8,128)(2,1)S(1)} %convolution_convert_fusion), channel_id=1, source_target_pairs={{0,2},{2,0},{4,6},{6,4},{8,10},{10,8},{12,14},{14,12},{16,18},{18,... | collective-permute-start | bytes 1032200 | tf_op jit(solution)/shard_map/ppermute | solution.py:21
  71.3 15.2 %copy-start.2 = (bf16[1,512,3584]{2,1,0:T(8,128)(2,1)S(1)}, bf16[1,512,3584]{2,1,0:T(8,128)(2,1)}, u32[]{:S(2)}) copy-start(bf16[1,512,3584]{2,1,0:T(8,128)(2,1)} %param.9) | copy-start | bytes 11010052
  71.3 15.1 %collective-permute-start.5 = (bf16[64,3584]{1,0:T(8,128)(2,1)S(1)}, bf16[64,3584]{1,0:T(8,128)(2,1)S(1)}, u32[]{:S(2)}, u32[]{:S(2)}) collective-permute-start(bf16[64,3584]{1,0:T(8,128)(2,1)S(1)} %collective-permute-done.2), channel_id=1, source_target_pairs={{0,1},{1,0},{2,3},{3,2},{4,5},{5,4},{6,7},{7,6},{8,9},{9,8},{10,11... | collective-permute-start | bytes 1376264 | tf_op jit(solution)/shard_map/ppermute | solution.py:21
